TPU v7x, 256 devices: a whole 4x4x8 slice. The times are simulated.
256 devices in a mesh: expert: 64 (over z, x_lo, y), replica: 4 (over x_hi, core).
Axes of the slice: x: 4 (x_hi: 2, x_lo: 2; x = x_hi * 2 + x_lo), y: 4, z: 8, core: 2. Of those that a mesh axis runs over, the one named last changes fastest.
Arguments:
- mid_acts: bfloat16 [32768, 1024], P(('expert', 'replica')), may hold values from -6 to 6
- out_grad: bfloat16 [32768, 1024], P(('expert', 'replica')), may hold values from -6 to 6
- queries: bfloat16 [32768, 1024], P(('expert', 'replica')), may hold values from -45 to 45
- key_rows: bfloat16 [32768, 1024], P(('expert', 'replica')), may hold values from -6 to 6
- value_head_rows: bfloat16 [32768, 1024], P(('expert', 'replica')), may hold values from -6 to 6
- seq_lengths: int32 [256], P(('expert', 'replica')), may hold values from 32 to 128
- expert_ids: int32 [32768, 2], P(('expert', 'replica')), may hold values from 0 to 63, all different within a row
- gate_probs: bfloat16 [32768, 2], P(('expert', 'replica')), may hold values from 0.049804688 to 0.94921875
- wide_in: bfloat16 [64, 1024, 4096], P('expert', None, 'replica'), may hold values from -0.1875 to 0.1875
- wide_out: bfloat16 [64, 4096, 1024], P('expert', 'replica'), may hold values from -0.09375 to 0.09375
- attn_proj: bfloat16 [1024, 1024], replicated, may hold values from -0.1875 to 0.1875
Outputs:
- grad_mid: bfloat16 [32768, 1024], P(('expert', 'replica'))
- grad_queries: bfloat16 [32768, 1024], P(('expert', 'replica'))
- grad_keys: bfloat16 [32768, 1024], P(('expert', 'replica'))
- grad_values: bfloat16 [32768, 1024], P(('expert', 'replica'))
- grad_gates: float32 [32768, 2], P(('expert', 'replica'))
- grad_wide_in: bfloat16 [64, 1024, 4096], P('expert', None, 'replica')
- grad_wide_out: bfloat16 [64, 4096, 1024], P('expert', 'replica')
- grad_proj: bfloat16 [1024, 1024], P('expert', 'replica')
Inputs may be any that keep to these rules, and one draw needn't show every extreme that they name: `expert_ids`: each token names two different experts.
All inputs are finite; a program needn't handle non-finite values.
Results may differ from a plain program's by a relative error of at most 0.015.
Values may be sent and summed in bfloat16 or wider, within the bound.
A program may use at most 192 MiB of HBM per device.

v0:
```python
import math

import jax
import jax.numpy as jnp
from jax import lax
from jax.sharding import PartitionSpec as P

HEAD_SIZE = 64


GELU_C = 0.7978845608028654
GELU_A = 0.044715


def gelu_tanh(pre):
    return 0.5 * pre * (1.0 + jnp.tanh(GELU_C * (pre + GELU_A * pre * pre * pre)))


def gelu_slope(pre):
    inner = jnp.tanh(GELU_C * (pre + GELU_A * pre * pre * pre))
    return 0.5 * (1.0 + inner) + 0.5 * pre * (1.0 - inner * inner) * GELU_C * (
        1.0 + 3.0 * GELU_A * pre * pre
    )


def group_slots(choices, experts, capacity):
    count = choices.shape[0]
    order = jnp.concatenate([choices[:, 0], choices[:, 1]])
    onehot = (order[:, None] == jnp.arange(experts, dtype=jnp.int32)[None, :]).astype(jnp.int32)
    before = jnp.cumsum(onehot, axis=0) - onehot
    place = jnp.sum(before * onehot, axis=1)
    place = jnp.where(place < capacity, place, -1)
    return jnp.stack([place[:count], place[count:]], axis=1)


def contract_rows(left, right):
    return lax.dot_general(
        left, right, (((0,), (0,)), ((), ())), preferred_element_type=jnp.float32
    )


def contract_cols(left, right):
    return lax.dot_general(
        left, right, (((1,), (1,)), ((), ())), preferred_element_type=jnp.float32
    )


def expert_backward(rows_x, rows_g, rows_gate, w_in, w_out):
    pre = jnp.dot(rows_x, w_in, preferred_element_type=jnp.float32)
    act = gelu_tanh(pre).astype(jnp.bfloat16)
    scaled = (rows_gate.astype(jnp.float32)[:, None] * rows_g.astype(jnp.float32)).astype(
        jnp.bfloat16
    )
    d_pre = (contract_cols(scaled, w_out) * gelu_slope(pre)).astype(jnp.bfloat16)
    grad_in = contract_rows(rows_x, d_pre)
    grad_out = contract_rows(act, scaled)
    slot_dx = contract_cols(d_pre, w_in)
    slot_out = jnp.dot(act, w_out, preferred_element_type=jnp.float32)
    return (grad_in, grad_out, slot_dx, slot_out)


def local_attention(queries, key_rows, value_head_rows, d_heads, seq_lengths):
    count = seq_lengths.shape[0]
    sequence_extent = queries.shape[0] // count
    head_split_rows = queries.shape[1] // HEAD_SIZE
    scale = 1.0 / math.sqrt(HEAD_SIZE)
    contraction_spec = (count, sequence_extent, head_split_rows, HEAD_SIZE)
    qmat = queries.reshape(contraction_spec)
    kmat = key_rows.reshape(contraction_spec)
    value_matrix = value_head_rows.reshape(contraction_spec)
    grad_value_matrix = d_heads.reshape(contraction_spec)
    scores = jnp.einsum("afcy,awcy->acfw", qmat, kmat, preferred_element_type=jnp.float32) * scale
    live = jnp.arange(sequence_extent, dtype=jnp.int32)[None, :] < seq_lengths[:, None]
    scores = jnp.where(live[:, None, None, :], scores, -1000000000.0)
    top = jnp.max(scores, axis=-1, keepdims=True)
    expo = jnp.exp(scores - top)
    probs = expo / jnp.sum(expo, axis=-1, keepdims=True)
    batched_probabilities = probs.astype(jnp.bfloat16)
    attention_mixture = jnp.einsum(
        "sfwn,snfy->swfy", batched_probabilities, value_matrix, preferred_element_type=jnp.float32
    ).astype(jnp.bfloat16)
    grad_probabilities = jnp.einsum(
        "afcy,awcy->acfw", grad_value_matrix, value_matrix, preferred_element_type=jnp.float32
    )
    grad_v = jnp.einsum(
        "bhqk,bqhd->bkhd",
        batched_probabilities,
        grad_value_matrix,
        preferred_element_type=jnp.float32,
    ).astype(jnp.bfloat16)
    inner = jnp.sum(grad_probabilities * probs, axis=-1, keepdims=True)
    dscore = (probs * (grad_probabilities - inner)).astype(jnp.bfloat16)
    grad_q = (
        jnp.einsum("sfwn,snfy->swfy", dscore, kmat, preferred_element_type=jnp.float32) * scale
    ).astype(jnp.bfloat16)
    grad_k = (
        jnp.einsum("bhqk,bqhd->bkhd", dscore, qmat, preferred_element_type=jnp.float32) * scale
    ).astype(jnp.bfloat16)
    flat = (count * sequence_extent, head_split_rows * HEAD_SIZE)
    return (
        grad_q.reshape(flat),
        grad_k.reshape(flat),
        grad_v.reshape(flat),
        attention_mixture.reshape(flat),
    )


def on_device(
    mid_acts,
    out_grad,
    queries,
    key_rows,
    value_head_rows,
    seq_lengths,
    expert_ids,
    gate_probs,
    wide_in,
    wide_out,
    attn_proj,
):
    tok_count, width = mid_acts.shape
    experts = lax.axis_size("expert")
    capacity = (5 * tok_count + 2 * experts - 1) // (2 * experts)
    slots = group_slots(expert_ids, experts, capacity)
    columns = jnp.arange(experts * capacity, dtype=jnp.int32)
    target = expert_ids * capacity + slots
    chosen = (target[:, :, None] == columns[None, None, :]) & (slots[:, :, None] >= 0)
    chosen_f = chosen.astype(jnp.float32)
    table = jnp.sum(chosen.astype(jnp.bfloat16), axis=1)
    slot_x = contract_rows(table, mid_acts).astype(jnp.bfloat16).reshape(experts, capacity, width)
    slot_g = contract_rows(table, out_grad).astype(jnp.bfloat16).reshape(experts, capacity, width)
    slot_gate = (
        jnp.einsum(
            "tkc,tk->c", chosen_f, gate_probs.astype(jnp.float32), precision=lax.Precision.HIGHEST
        )
        .astype(jnp.bfloat16)
        .reshape(experts, capacity)
    )
    sent_x, sent_g, sent_gate = (
        lax.all_to_all(slot_x, "expert", split_axis=0, concat_axis=0, tiled=True),
        lax.all_to_all(slot_g, "expert", split_axis=0, concat_axis=0, tiled=True),
        lax.all_to_all(slot_gate, "expert", split_axis=0, concat_axis=0, tiled=True),
    )
    w_in = wide_in[0]
    w_out = wide_out[0]
    all_x, all_g, all_gate = (
        lax.all_gather(sent_x, "replica", axis=0, tiled=True),
        lax.all_gather(sent_g, "replica", axis=0, tiled=True),
        lax.all_gather(sent_gate, "replica", axis=0, tiled=True),
    )
    grad_in, grad_out, term_dx, term_side = expert_backward(
        all_x.reshape(-1, width), all_g.reshape(-1, width), all_gate.reshape(-1), w_in, w_out
    )
    slot_dx, side = (
        lax.psum_scatter(term_dx, "replica", scatter_dimension=0, tiled=True),
        lax.psum_scatter(term_side, "replica", scatter_dimension=0, tiled=True),
    )
    back_dx = slot_dx.reshape(experts, capacity, width)
    back_side = side.reshape((experts, capacity) + side.shape[1:])
    home_dx, home_side = (
        lax.all_to_all(back_dx, "expert", split_axis=0, concat_axis=0, tiled=True),
        lax.all_to_all(back_side, "expert", split_axis=0, concat_axis=0, tiled=True),
    )
    out_f = out_grad.astype(jnp.float32)
    moe_dx = jnp.dot(
        table.astype(jnp.float32), home_dx.reshape(-1, width), precision=lax.Precision.HIGHEST
    )
    picked = jnp.einsum(
        "tkc,cd->tkd", chosen_f, home_side.reshape(-1, width), precision=lax.Precision.HIGHEST
    )
    grad_gates = jnp.sum(picked * out_f[:, None, :], axis=2)
    grad_mid = (out_f + moe_dx).astype(jnp.bfloat16)
    d_heads = contract_cols(grad_mid, attn_proj).astype(jnp.bfloat16)
    grad_q, grad_k, grad_v, attention_mixture = local_attention(
        queries, key_rows, value_head_rows, d_heads, seq_lengths
    )
    proj_term = contract_rows(attention_mixture, grad_mid)
    proj_part = lax.psum_scatter(proj_term, "expert", scatter_dimension=0, tiled=True)
    proj_part = lax.psum_scatter(
        proj_part.astype(jnp.bfloat16), "replica", scatter_dimension=1, tiled=True
    ).astype(jnp.float32)
    return (
        grad_mid,
        grad_q,
        grad_k,
        grad_v,
        grad_gates,
        grad_in.astype(jnp.bfloat16)[None],
        grad_out.astype(jnp.bfloat16)[None],
        proj_part.astype(jnp.bfloat16),
    )


def solution(mesh):
    placed = (
        P(("expert", "replica"), None),
        P(("expert", "replica"), None),
        P(("expert", "replica"), None),
        P(("expert", "replica"), None),
        P(("expert", "replica"), None),
        P(("expert", "replica")),
        P(("expert", "replica"), None),
        P(("expert", "replica"), None),
        P("expert", None, "replica"),
        P("expert", "replica", None),
        P(),
    )
    return jax.shard_map(
        on_device,
        mesh=mesh,
        in_specs=placed,
        out_specs=(
            P(("expert", "replica"), None),
            P(("expert", "replica"), None),
            P(("expert", "replica"), None),
            P(("expert", "replica"), None),
            P(("expert", "replica"), None),
            P("expert", None, "replica"),
            P("expert", "replica", None),
            P("expert", "replica"),
        ),
        check_vma=False,
    )
```

profile of v0, /device:TPU:4, one launch (start us, length us, event | category | flops | bytes accessed | tf_op | source)
XLA Modules:
  0.0 665.6 jit_solution(11712012931834005283)
XLA Ops:
  9.9 2.1 convolution_convert_fusion
  13.3 40.7 %all_to_all.33 = bf16[64,5,1024]{2,1,0:T(8,128)(2,1)S(1)} all-to-all(bf16[64,5,1024]{2,1,0:T(8,128)(2,1)S(1)} %reshape.194), channel_id=1, replica_groups=mesh['expert'=64,'replica'=4] {'expert'}, dimensions={0} | all-to-all | bytes 1310720 | tf_op jit(solution)/shard_map/all_to_all | solution.py:140
  57.8 33.5 %all_to_all.34 = bf16[64,5,1024]{2,1,0:T(8,128)(2,1)S(1)} all-to-all(bf16[64,5,1024]{2,1,0:T(8,128)(2,1)S(1)} %reshape.193), channel_id=1, replica_groups=mesh['expert'=64,'replica'=4] {'expert'}, dimensions={0} | all-to-all | bytes 1310720 | tf_op jit(solution)/shard_map/all_to_all | solution.py:141
  93.1 16.9 %all_to_all.35 = bf16[64,1,5]{2,1,0:T(2,128)(2,1)S(1)} all-to-all(bf16[64,1,5]{2,1,0:T(2,128)(2,1)S(1)} %all_to_all.27), channel_id=1, replica_groups=mesh['expert'=64,'replica'=4] {'expert'}, dimensions={0} | all-to-all | bytes 1280 | tf_op jit(solution)/shard_map/all_to_all | solution.py:142
  110.0 7.8 %all-gather = bf16[256,1,5]{2,1,0:T(2,128)(2,1)S(1)} all-gather(bf16[64,1,5]{2,1,0:T(2,128)(2,1)S(1)} %all_to_all.35), channel_id=2, replica_groups=mesh['expert'=64,'replica'=4] {'replica'}, dimensions={0}, use_global_device_ids=true | all-gather | bytes 3200 | tf_op jit(solution)/shard_map/all_gather | solution.py:149
  118.6 5.3 copy.71
  123.9 6.2 reshape.195
  130.1 2.2 multiply_convert_fusion.2
  132.4 3.5 copy.69
  135.9 6.2 convert_element_type.142
  142.1 4.8 fusion.12
  146.9 5.8 fusion.7
  154.3 4.7 fusion.10
  160.6 8.5 %fusion.14 = f32[1280,1024]{1,0:T(8,128)} fusion(bf16[1,1024,1024]{2,1,0:T(8,128)(2,1)S(1)} %copy-done.21, f32[1280,1024]{1,0:T(8,128)} %copy-done.23), kind=kOutput, calls=%fused_computation.19 | convolution fusion | flops 2696151040 | bytes 12582912 | tf_op jit(solution)/shard_map/dot_general | solution.py:58
  169.1 48.4 %reduce-scatter.5.cloned.1.call-done = f32[320,1024]{1,0:T(8,128)} async-done(((f32[1280,1024]{1,0:T(8,128)}), f32[320,1024]{1,0:T(8,128)}) %reduce-scatter.5.cloned.1.call-update) | async-done | bytes 1310736 | tf_op jit(solution)/shard_map/reduce_scatter | solution.py:155
  217.5 2.6 reshape.196
  220.1 12.2 %all-to-all-start.3 = ((f32[64,5,1024]{2,1,0:T(8,128)}), f32[64,5,1024]{2,1,0:T(8,128)S(1)}, u32[]{:S(2)}, u32[]{:S(2)}) async-start(f32[64,5,1024]{2,1,0:T(8,128)} %reshape.196), calls=%async_computation.4 | async-start | bytes 4194304 | tf_op jit(solution)/shard_map/all_to_all | solution.py:161
  236.6 46.2 %all-to-all-done.3 = f32[64,5,1024]{2,1,0:T(8,128)S(1)} async-done(((f32[64,5,1024]{2,1,0:T(8,128)}), f32[64,5,1024]{2,1,0:T(8,128)S(1)}, u32[]{:S(2)}, u32[]{:S(2)}) %all-to-all-start.3) | async-done | bytes 1310752 | tf_op jit(solution)/shard_map/all_to_all | solution.py:161
  284.7 3.8 fusion.45
  288.5 6.2 reduce-scatter.7.cloned.1.call-done
  294.8 2.6 reshape.205
  297.4 11.7 %all-to-all-start.4 = ((f32[64,5,1024]{2,1,0:T(8,128)}), f32[64,5,1024]{2,1,0:T(8,128)S(1)}, u32[]{:S(2)}, u32[]{:S(2)}) async-start(f32[64,5,1024]{2,1,0:T(8,128)} %reshape.205), calls=%async_computation.6 | async-start | bytes 4194304 | tf_op jit(solution)/shard_map/all_to_all | solution.py:162
  310.6 6.6 copy.79
  317.2 8.3 %reshape.209 = f32[1280,1024]{1,0:T(8,128)} reshape(f32[256,5,1024]{2,1,0:T(8,128)} %copy.79) | data formatting | bytes 10485760 | tf_op jit(solution)/shard_map/convert_element_type | solution.py:51
  325.5 7.0 %convert_bitcast_fusion.1 = bf16[1,1024,1024]{2,1,0:T(8,128)(2,1)} fusion(bf16[1280,1024]{1,0:T(8,128)(2,1)} %reshape.195, bf16[1280,1024]{1,0:T(8,128)(2,1)} %copy-done.24), kind=kOutput, calls=%fused_computation.23 | convolution fusion | flops 2685403136 | bytes 7340032 | tf_op jit(solution)/shard_map/dot_general | solution.py:37
  332.4 7.7 %convert_bitcast_fusion = bf16[1,1024,1024]{2,1,0:T(8,128)(2,1)} fusion(f32[1280,1024]{1,0:T(8,128)S(1)} %copy-done.2, f32[1280]{0:T(1024)S(1)} %reshape.208, f32[1280,1024]{1,0:T(8,128)} %copy-done.23), kind=kOutput, calls=%fused_computation.22 | convolution fusion | flops 2699821056 | bytes 12588032 | tf_op jit(solution)/shard_map/dot_general | solution.py:37
  341.9 19.1 %all-to-all-done.4 = f32[64,5,1024]{2,1,0:T(8,128)S(1)} async-done(((f32[64,5,1024]{2,1,0:T(8,128)}), f32[64,5,1024]{2,1,0:T(8,128)S(1)}, u32[]{:S(2)}, u32[]{:S(2)}) %all-to-all-start.4) | async-done | bytes 1310752 | tf_op jit(solution)/shard_map/all_to_all | solution.py:162
  361.2 2.6 convolution_convert_fusion.3
  363.8 1.9 multiply_reduce_fusion
  368.1 260.4 %reduce-scatter.9.cloned.1.call-done = f32[16,1024]{1,0:T(8,128)} async-done(((f32[1024,1024]{1,0:T(8,128)}), f32[16,1024]{1,0:T(8,128)}) %reduce-scatter.9.cloned.1.call-update) | async-done | bytes 65552 | tf_op jit(solution)/shard_map/reduce_scatter | solution.py:178
  630.0 2.8 fusion.20
  638.2 20.1 %reduce-scatter.11.cloned.1.call-done = bf16[16,256]{1,0:T(8,128)(2,1)} async-done(((bf16[16,1024]{1,0:T(8,128)(2,1)}), bf16[16,256]{1,0:T(8,128)(2,1)}) %reduce-scatter.11.cloned.1.call-update) | async-done | bytes 8208 | tf_op jit(solution)/shard_map/reduce_scatter | solution.py:179
  (107 shorter events, 31.6 us)
Async XLA Ops:
  7.2 134.9 %copy-start = (bf16[1,1024,1024]{2,1,0:T(8,128)(2,1)S(1)}, bf16[1,1024,1024]{2,1,0:T(8,128)(2,1)}, u32[]{:S(2)}) copy-start(bf16[1,1024,1024]{2,1,0:T(8,128)(2,1)} %param.19) | copy-start | bytes 6291460
  7.2 48.2 %copy-start.6 = (bf16[128,1024]{1,0:T(8,128)(2,1)S(1)}, bf16[128,1024]{1,0:T(8,128)(2,1)}, u32[]{:S(2)}) copy-start(bf16[128,1024]{1,0:T(8,128)(2,1)} %param.12) | copy-start | bytes 786436
  7.2 111.4 %all-gather.6.cloned.1.call-start = ((), (), s32[]{:S(2)}) async-start(), calls=%async_computation.10 | async-start | bytes 3276800 | tf_op jit(solution)/shard_map/all_gather | solution.py:147
  55.3 37.5 %copy-start.22 = (bf16[128,2]{0,1:T(2,128)(2,1)S(1)}, bf16[128,2]{0,1:T(2,128)(2,1)}, u32[]{:S(2)}) copy-start(bf16[128,2]{0,1:T(2,128)(2,1)} %param.18) | copy-start | bytes 1540
  55.3 74.8 %all-gather.4.cloned.1.call-start = ((), (), s32[]{:S(2)}) async-start(), calls=%async_computation.9 | async-start | bytes 3276800 | tf_op jit(solution)/shard_map/all_gather | solution.py:148
  92.7 124.8 %reduce-scatter.5.cloned.1.call-start = ((), (), s32[]{:S(2)}) async-start(), calls=%async_computation.11 | async-start | bytes 6553600 | tf_op jit(solution)/shard_map/reduce_scatter | solution.py:155
  142.1 4.8 copy-start.3
  142.1 4.8 copy-start.20
  146.9 5.8 copy-start.23
  152.7 1.6 copy-start.24
  159.0 1.6 copy-start.21
  159.0 135.7 %reduce-scatter.7.cloned.1.call-start = ((), (), s32[]{:S(2)}) async-start(), calls=%async_computation.12 | async-start | bytes 6553600 | tf_op jit(solution)/shard_map/reduce_scatter | solution.py:156
  169.1 64.0 %copy-start.16 = (bf16[128,1024]{1,0:T(8,128)(2,1)S(1)}, bf16[128,1024]{1,0:T(8,128)(2,1)}, u32[]{:S(2)}) copy-start(bf16[128,1024]{1,0:T(8,128)(2,1)} %param.13) | copy-start | bytes 786436
  169.1 64.1 %copy-start.17 = (bf16[128,1024]{1,0:T(8,128)(2,1)S(1)}, bf16[128,1024]{1,0:T(8,128)(2,1)}, u32[]{:S(2)}) copy-start(bf16[128,1024]{1,0:T(8,128)(2,1)} %param.14) | copy-start | bytes 786436
  169.1 64.3 %copy-start.18 = (bf16[128,1024]{1,0:T(8,128)(2,1)S(1)}, bf16[128,1024]{1,0:T(8,128)(2,1)}, u32[]{:S(2)}) copy-start(bf16[128,1024]{1,0:T(8,128)(2,1)} %param.15) | copy-start | bytes 786436
  220.1 62.7 %all-to-all-start.3 = ((f32[64,5,1024]{2,1,0:T(8,128)}), f32[64,5,1024]{2,1,0:T(8,128)S(1)}, u32[]{:S(2)}, u32[]{:S(2)}) async-start(f32[64,5,1024]{2,1,0:T(8,128)} %reshape.196), calls=%async_computation.4 | async-start | bytes 4194304 | tf_op jit(solution)/shard_map/all_to_all | solution.py:161
  232.4 396.2 %reduce-scatter.9.cloned.1.call-start = ((), (), s32[]{:S(2)}) async-start(), calls=%async_computation.13 | async-start | bytes 4259840 | tf_op jit(solution)/shard_map/reduce_scatter | solution.py:178
  233.3 3.4 copy-start.14
  233.4 3.2 copy-start.12
  233.6 3.0 copy-start.19
  284.7 3.8 copy-start.4
  288.5 20.6 %copy-start.7 = (bf16[128,1024]{1,0:T(8,128)(2,1)S(1)}, bf16[128,1024]{1,0:T(8,128)(2,1)}, u32[]{:S(2)}) copy-start(bf16[128,1024]{1,0:T(8,128)(2,1)} %param.12) | copy-start | bytes 786436
  288.5 21.5 %copy-start.10 = (bf16[256,1,5]{2,1,0:T(2,128)(2,1)S(1)}, bf16[256,1,5]{2,1,0:T(2,128)(2,1)}, u32[]{:S(2)}) copy-start(bf16[256,1,5]{2,1,0:T(2,128)(2,1)} %copy-done.9) | copy-start | bytes 7684
  297.4 63.6 %all-to-all-start.4 = ((f32[64,5,1024]{2,1,0:T(8,128)}), f32[64,5,1024]{2,1,0:T(8,128)S(1)}, u32[]{:S(2)}, u32[]{:S(2)}) async-start(f32[64,5,1024]{2,1,0:T(8,128)} %reshape.205), calls=%async_computation.6 | async-start | bytes 4194304 | tf_op jit(solution)/shard_map/all_to_all | solution.py:162
  309.1 349.2 %reduce-scatter.11.cloned.1.call-start = ((), (), s32[]{:S(2)}) async-start(), calls=%async_computation.14 | async-start | bytes 40960 | tf_op jit(solution)/shard_map/reduce_scatter | solution.py:179
  325.5 7.0 %copy-start.2 = (f32[1280,1024]{1,0:T(8,128)S(1)}, f32[1280,1024]{1,0:T(8,128)}, u32[]{:S(2)}) copy-start(f32[1280,1024]{1,0:T(8,128)} %reshape.209) | copy-start | bytes 15728644
  332.4 7.8 %copy-start.5 = (bf16[128,1024]{1,0:T(8,128)(2,1)S(1)}, bf16[128,1024]{1,0:T(8,128)(2,1)}, u32[]{:S(2)}) copy-start(bf16[128,1024]{1,0:T(8,128)(2,1)} %copy-done.4) | copy-start | bytes 786436
  332.4 7.8 %copy-start.8 = (bf16[1024,1024]{1,0:T(8,128)(2,1)S(1)}, bf16[1024,1024]{1,0:T(8,128)(2,1)}, u32[]{:S(2)}) copy-start(bf16[1024,1024]{1,0:T(8,128)(2,1)} %param.21) | copy-start | bytes 6291460
  363.8 1.9 copy-start.11
  363.8 2.1 copy-start.15
  363.8 3.3 copy-start.13
  363.8 294.5 %copy-start.1 = (bf16[1,1024,1024]{2,1,0:T(8,128)(2,1)S(1)}, bf16[1,1024,1024]{2,1,0:T(8,128)(2,1)}, u32[]{:S(2)}) copy-start(bf16[1,1024,1024]{2,1,0:T(8,128)(2,1)} %param.19) | copy-start | bytes 6291460
  (1 other events, 0.6 us)
Sparse Core Ops, SparseCore 0:
  55.4 37.2 all-gather.5
  95.1 31.1 all-gather.3
  159.2 58.3 reduce-scatter.4
  220.4 74.3 reduce-scatter.6
  297.1 331.3 reduce-scatter.8
  631.8 26.4 reduce-scatter.10
where the time goes:
time: 674 us; the launch traced here: 666 us
  waiting for transfers between devices  400 us (59%)
  blocking collectives  98.9 us (15%)
  matrix products  60.6 us (9%)
  local copies, waits for them, and re-layouts  58.8 us (9%)
  starting transfers between devices  24.4 us (4%)
  between operations  15.6 us (2%)
  other arithmetic  6.8 us (1%)
    reduce_scatter x1, waiting for transfers between devices, on_device(): lax.psum_scatter(proj_term, 'expert', scatter_dimension=0, tiled=True)  260 us
    reduce_scatter x1, waiting for transfers between devices, on_device(): lax.psum_scatter(term_dx, 'replica', scatter_dimension=0, tiled=True)  48.4 us
    all_to_all x1, waiting for transfers between devices, on_device(): lax.all_to_all(back_dx, 'expert', split_axis=0, concat_axis=0, tiled=True)  46.2 us
    all_to_all x1, blocking collectives, on_device(): lax.all_to_all(slot_x, 'expert', split_axis=0, concat_axis=0, tiled=True)  40.7 us
    all_to_all x1, blocking collectives, on_device(): lax.all_to_all(slot_g, 'expert', split_axis=0, concat_axis=0, tiled=True)  33.5 us
    dot_general x5, matrix products, contract_rows(): lax.dot_general(left, right, (((0,), (0,)), ((), ())), preferred_element_...  21.7 us
    reduce_scatter x1, waiting for transfers between devices, on_device(): lax.psum_scatter(proj_part.astype(jnp.bfloat16), 'replica', scatter_dimen...  20.1 us
    all_to_all x1, waiting for transfers between devices, on_device(): lax.all_to_all(back_side, 'expert', split_axis=0, concat_axis=0, tiled=True)  19.1 us
  transfers between devices with their start and end apart: 8, of which 6 were waited for; matrix products, arithmetic and copies ran while one was open for 13% of the time, Pallas kernels for 0%

commit v1 on v0

v1 whole, which is shorter than its diff:
```python
import math

import jax
import jax.numpy as jnp
import numpy as np
from jax import lax
from jax.experimental import pallas as pl
from jax.experimental.pallas import tpu as pltpu
from jax.sharding import PartitionSpec as P

HEAD_SIZE = 64
GELU_C = 0.7978845608028654
GELU_A = 0.044715
MESH = pl.DeviceIdType.MESH

NZ, NQ, NP = 8, 8, 16
CAP = 5
TOK = 128
D = 1024
ROWS = 2 * NQ * CAP
ALL = NZ * ROWS
KC, CW = 4, 256
HALF = D // 2
EXT = HALF + 128
BLK = 4 * ROWS
F32 = jnp.float32
BF16 = jnp.bfloat16


def group_slots(choices, experts, capacity):
    count = choices.shape[0]
    order = jnp.concatenate([choices[:, 0], choices[:, 1]])
    onehot = (order[:, None] == jnp.arange(experts, dtype=jnp.int32)[None, :]).astype(jnp.int32)
    before = jnp.cumsum(onehot, axis=0) - onehot
    place = jnp.sum(before * onehot, axis=1)
    place = jnp.where(place < capacity, place, -1)
    return place.reshape(2, count)


def dot_nn(a, b):
    return jnp.dot(a, b, preferred_element_type=F32)


def dot_nt(a, b):
    return lax.dot_general(a, b, (((1,), (1,)), ((), ())), preferred_element_type=F32)


def dot_tn(a, b):
    return lax.dot_general(a, b, (((0,), (0,)), ((), ())), preferred_element_type=F32)


def swap_table():
    out = np.arange(ALL)
    z, rest = out // ROWS, out % ROWS
    core, rest = rest // (NQ * CAP), rest % (NQ * CAP)
    q, s = rest // CAP, rest % CAP
    table = np.zeros((ALL, ALL), np.float32)
    table[out, q * ROWS + core * NQ * CAP + z * CAP + s] = 1.0
    return table


def moe_kernel(
    rowidx, gate, x_ref, g_ref, mixt, swap, w_in_hbm, w_out_hbm,
    mid, gates, grad_in, grad_out, proj,
    w_in, w_out, m_buf, m_send, t_buf, t_use, sa, ra, sb, rr,
    pre, dact, act, dpre, side, ds, dr, do, sbr, rbr, yy, sar, rar, fs, fr,
    rs_s, rs_r, rs_o, rs_b, rs2, rs_c, rs3,
    w_sem, m_ss, m_rs, t_ss, t_rs, a_ss, a_rs, b_ss, b_rs, c_ss, c_rs,
    cr_ss, cr_rs, br_ss, br_rs, ar_ss, ar_rs, f_ss, f_rs, p1_ss, p1_rs, p2_ss, p2_rs, p3_ss, p3_rs,
):
    e = lax.axis_index("expert")
    r = lax.axis_index("replica")
    z, q, xh, c = e // NQ, e % NQ, r // 2, r % 2
    pm = xh * NQ + q
    other = 1 - c
    partner = (e, xh * 2 + other)

    def dev_z(j):
        return (((z + j) % NZ) * NQ + q, r)

    def plane_of(j):
        return (pm + j) % NP

    def dev_p(j):
        p = plane_of(j)
        return (z * NQ + p % NQ, (p // NQ) * 2 + c)

    def remote(src, dst, ss, rs, dev):
        return pltpu.make_async_remote_copy(
            src_ref=src, dst_ref=dst, send_sem=ss, recv_sem=rs, device_id=dev, device_id_type=MESH
        )

    load_in = pltpu.make_async_copy(w_in_hbm, w_in, w_sem.at[0])
    load_out = pltpu.make_async_copy(w_out_hbm, w_out, w_sem.at[1])
    load_in.start()
    load_out.start()

    bar = pltpu.get_barrier_semaphore()

    def greet_z(j, _):
        pl.semaphore_signal(bar, inc=1, device_id=dev_z(j), device_id_type=MESH)
        return 0

    def greet_p(j, _):
        pl.semaphore_signal(bar, inc=1, device_id=dev_p(j), device_id_type=MESH)
        return 0

    pl.semaphore_signal(bar, inc=1, device_id=partner, device_id_type=MESH)
    lax.fori_loop(1, NZ, greet_z, 0)
    lax.fori_loop(1, NP, greet_p, 0)

    rows_of = lax.broadcasted_iota(jnp.int32, (ALL, TOK), 0)
    signed = jnp.where(rows_of == rowidx[0:1, :], gate[0:1, :], 0.0) - jnp.where(
        rows_of == rowidx[1:2, :], gate[1:2, :], 0.0
    )
    t_buf[c] = signed.astype(BF16)

    @pl.when(c == 0)
    def _():
        m_buf[0] = x_ref[...]
        m_send[...] = g_ref[...]

    @pl.when(c == 1)
    def _():
        m_buf[1] = g_ref[...]
        m_send[...] = x_ref[...]

    pl.semaphore_wait(bar, NZ + NP - 1)

    m_copy = remote(m_send, m_buf.at[c], m_ss, m_rs, partner)
    t_copy = remote(t_buf.at[c], t_buf.at[c], t_ss, t_rs, partner)
    t_copy.start()
    m_copy.start()
    t_copy.wait_recv()
    for j in range(2):
        size = jnp.abs(t_buf[j].astype(F32))
        t_use[j] = jnp.where(c == 0, jnp.where(size > 0.0, 1.0, 0.0), size).astype(BF16)
    m_copy.wait_recv()

    def copy_a(k, j):
        return remote(sa.at[k, j], ra.at[k, (NZ - j) % NZ], a_ss.at[k, j], a_rs.at[k, (NZ - j) % NZ], dev_z(j))

    def recv_a(k, j):
        return remote(sa.at[k, j], ra.at[k, j], a_ss.at[k, j], a_rs.at[k, j], dev_z(j))

    def copy_b(k, j):
        return remote(
            sb.at[k, plane_of(j) % NQ], rr.at[c, k, (NP - j) % NP], b_ss.at[k, j], b_rs.at[k, (NP - j) % NP], dev_p(j)
        )

    def recv_b(k, j):
        return remote(sb.at[k, 0], rr.at[c, k, j], b_ss.at[k, j], b_rs.at[k, j], dev_p(j))

    def copy_c(k):
        return remote(rr.at[c, k], rr.at[c, k], c_ss.at[k], c_rs.at[k], partner)

    def recv_c(k):
        return remote(rr.at[other, k], rr.at[other, k], c_ss.at[k], c_rs.at[k], partner)

    def each(count, body):
        def step(j, _):
            body(j)
            return 0

        lax.fori_loop(1, count, step, 0)

    for k in range(KC):
        cols = slice(k * CW, (k + 1) * CW)
        rows = dot_nn(t_use[0], m_buf[0, :, cols]) + dot_nn(t_use[1], m_buf[1, :, cols])
        sa[k] = rows.astype(BF16).reshape(NZ, ROWS, CW)
        each(NZ, lambda j: copy_a(k, j).start())
        ra[k, 0] = sa[k, 0]

    def stage_b(k):
        each(NZ, lambda j: recv_a(k, j).wait_recv())
        rows = dot_nn(swap[...], ra[k].reshape(ALL, CW))
        sb[k] = rows.astype(BF16).reshape(NQ, ROWS, CW)
        each(NP, lambda j: copy_b(k, j).start())
        rr[c, k, 0] = sb[k, q]

    def stage_c(k):
        each(NP, lambda j: recv_b(k, j).wait_recv())
        copy_c(k).start()

    def stage_d(k):
        recv_c(k).wait_recv()
        if k == 0:
            load_in.wait()
            load_out.wait()

        def body(i, _):
            xk = rr[0, k, pl.ds(4 * i, 4)].reshape(BLK, CW)
            gk = rr[1, k, pl.ds(4 * i, 4)].reshape(BLK, CW)
            p_new = dot_nn(xk, w_in[k * CW : (k + 1) * CW, :])
            d_new = dot_nt(gk, w_out[:, k * CW : (k + 1) * CW])
            if k == 0:
                pre[i] = p_new
                dact[i] = d_new
            else:
                pre[i] += p_new
                dact[i] += d_new
            return 0

        lax.fori_loop(0, 4, body, 0)

    for step in range(KC + 2):
        if step < KC:
            stage_b(step)
        if 0 <= step - 1 < KC:
            stage_c(step - 1)
        if 0 <= step - 2 < KC:
            stage_d(step - 2)

    SUB = 32
    lanes = lax.broadcasted_iota(jnp.int32, (SUB, 128), 1)

    def gelu_block(i):
        def body(n, _):
            at = pl.multiple_of(n * SUB, SUB)
            u = pre[i, pl.ds(at, SUB), :]
            da = dact[i, pl.ds(at, SUB), :]
            uu = u * u
            inner = jnp.tanh(GELU_C * (u + GELU_A * uu * u))
            half = 0.5 * (1.0 + inner)
            a = (u * half).astype(BF16)
            slope = half + 0.5 * u * (1.0 - inner * inner) * (GELU_C + (3.0 * GELU_A * GELU_C) * uu)
            dp = (da * slope).astype(BF16)
            s = jnp.sum(a.astype(F32) * da, axis=1, keepdims=True)
            hi = s.astype(BF16).astype(F32)
            to = pl.multiple_of(i * BLK + at, SUB)
            side[pl.ds(to, SUB), :] = jnp.where(lanes == 0, hi, jnp.where(lanes == 1, s - hi, 0.0)).astype(BF16)
            for f in range(KC):
                act[f, pl.ds(to, SUB), :] = a[:, f * CW : (f + 1) * CW]
                dpre[f, pl.ds(to, SUB), :] = dp[:, f * CW : (f + 1) * CW]
            return 0

        lax.fori_loop(0, BLK // SUB, body, 0)

    def dx_block(i):
        rows = pl.ds(i * BLK, BLK)

        def half_of(h):
            total = None
            for f in range(KC):
                term = dot_nt(
                    dpre[f, rows, :], w_in[pl.ds(pl.multiple_of(h * HALF, HALF), HALF), f * CW : (f + 1) * CW]
                )
                total = term if total is None else total + term
            return total

        ds[i] = half_of(other).astype(BF16).reshape(4, ROWS, HALF)
        copy_cr(i).start()
        do[i] = half_of(c)

    def copy_cr(i):
        return remote(ds.at[i], dr.at[i], cr_ss.at[i], cr_rs.at[i], partner)

    def copy_br(j):
        return remote(sbr.at[j], rbr.at[(NP - j) % NP], br_ss.at[j], br_rs.at[(NP - j) % NP], dev_p(j))

    def recv_br(j):
        return remote(sbr.at[j], rbr.at[j], br_ss.at[j], br_rs.at[j], dev_p(j))

    def return_block(i):
        copy_cr(i).wait_recv()
        for n in range(4):
            rows = slice(n * ROWS, (n + 1) * ROWS)
            sbr[4 * i + n, :, 0:HALF] = (do[i, rows, :] + dr[i, n].astype(F32)).astype(BF16)
            sbr[4 * i + n, :, HALF:EXT] = side[i * BLK + n * ROWS : i * BLK + (n + 1) * ROWS, :]
            if 4 * i + n:
                copy_br(4 * i + n).start()

    for i in range(5):
        if i < 4:
            gelu_block(i)
            dx_block(i)
        if i > 0:
            return_block(i - 1)

    def wide_in_body(n, _):
        at = pl.multiple_of((n // KC) * CW, CW)
        f = n % KC
        rows = rr[0, n // KC].reshape(NP * ROWS, CW)
        term = dot_tn(rows, dpre[f]).astype(BF16)
        grad_in[pl.ds(at, CW), pl.ds(pl.multiple_of(f * CW, CW), CW)] = term
        return 0

    def wide_out_body(n, _):
        f = n // KC
        k = n % KC
        rows = rr[1, k].reshape(NP * ROWS, CW)
        term = dot_tn(act[f], rows).astype(BF16)
        grad_out[pl.ds(pl.multiple_of(f * CW, CW), CW), pl.ds(pl.multiple_of(k * CW, CW), CW)] = term
        return 0

    lax.fori_loop(0, KC * KC, wide_in_body, 0)

    each(NP, lambda j: recv_br(j).wait_recv())
    lanes_r = lax.broadcasted_iota(jnp.int32, (ROWS, 128), 1)
    for j in range(NQ):
        one = sbr if j == 0 else rbr
        to = (q + j) % NQ
        yy[to, :, 0:HALF] = (one[j, :, 0:HALF].astype(F32) + rbr[j + NQ, :, 0:HALF].astype(F32)).astype(BF16)
        s = jnp.sum(
            one[j, :, HALF:EXT].astype(F32) + rbr[j + NQ, :, HALF:EXT].astype(F32), axis=1, keepdims=True
        )
        hi = s.astype(BF16).astype(F32)
        yy[to, :, HALF:EXT] = jnp.where(lanes_r == 0, hi, jnp.where(lanes_r == 1, s - hi, 0.0)).astype(BF16)
    sar[...] = dot_nn(swap[...], yy[...].reshape(ALL, EXT)).astype(BF16).reshape(NZ, ROWS, EXT)

    def copy_ar(j):
        return remote(sar.at[j], rar.at[(NZ - j) % NZ], ar_ss.at[j], ar_rs.at[(NZ - j) % NZ], dev_z(j))

    def recv_ar(j):
        return remote(sar.at[j], rar.at[j], ar_ss.at[j], ar_rs.at[j], dev_z(j))

    each(NZ, lambda j: copy_ar(j).start())
    rar[0] = sar[0]
    lax.fori_loop(0, KC * KC, wide_out_body, 0)
    each(NZ, lambda j: recv_ar(j).wait_recv())

    def home(j):
        t = t_buf[j].astype(F32)
        any_t = jnp.where(t != 0.0, 1.0, 0.0).astype(BF16)
        first = jnp.where(t > 0.0, 1.0, 0.0).astype(BF16)
        second = jnp.where(t < 0.0, 1.0, 0.0).astype(BF16)
        rows = rar[...].reshape(ALL, EXT)
        return (
            dot_tn(any_t, rows[:, 0:HALF]),
            dot_tn(first, rows[:, HALF:EXT]),
            dot_tn(second, rows[:, HALF:EXT]),
        )

    theirs = home(other)
    fs[:, 0:HALF] = theirs[0]
    fs[:, HALF : HALF + 128] = theirs[1]
    fs[:, HALF + 128 : HALF + 256] = theirs[2]
    f_copy = remote(fs, fr, f_ss, f_rs, partner)
    f_copy.start()
    ours = home(c)
    f_copy.wait_recv()
    mine_at = pl.ds(pl.multiple_of(c * HALF, HALF), HALF)
    other_at = pl.ds(pl.multiple_of(other * HALF, HALF), HALF)
    mid[:, mine_at] = (g_ref[:, mine_at].astype(F32) + ours[0]).astype(BF16)
    mid[:, other_at] = (g_ref[:, other_at].astype(F32) + fr[:, 0:HALF]).astype(BF16)
    gates[0] = ours[1] + fr[:, HALF : HALF + 128]
    gates[1] = ours[2] + fr[:, HALF + 128 : HALF + 256]

    def proj_cols(b, core):
        cols = pl.ds(pl.multiple_of(b * 512 + core * 256, 256), 256)
        return dot_nn(mixt[...], mid[:, cols])

    for b in range(2):
        rs_s[b] = proj_cols(b, other).astype(BF16).reshape(NZ, NQ, 16, 256)
    p1 = remote(rs_s, rs_r, p1_ss, p1_rs, partner)
    p1.start()
    for b in range(2):
        rs_o[b] = proj_cols(b, c).reshape(NZ, NQ, 16, 256)
    p1.wait_recv()
    for b in range(2):
        rs_b[b] = (rs_o[b] + rs_r[b].astype(F32)).astype(BF16)

    def copy_p2(j):
        p = plane_of(j)
        return remote(
            rs_b.at[p // NQ, :, p % NQ], rs2.at[(NP - j) % NP], p2_ss.at[j], p2_rs.at[(NP - j) % NP], dev_p(j)
        )

    def recv_p2(j):
        return remote(rs_b.at[0, :, 0], rs2.at[j], p2_ss.at[j], p2_rs.at[j], dev_p(j))

    each(NP, lambda j: copy_p2(j).start())
    rs2[0] = rs_b[xh, :, q]
    each(NP, lambda j: recv_p2(j).wait_recv())

    def add_p2(j, total):
        return total + rs2[j].astype(F32)

    rs_c[...] = lax.fori_loop(1, NP, add_p2, rs2[0].astype(F32)).astype(BF16)

    def copy_p3(j):
        return remote(
            rs_c.at[(z + j) % NZ], rs3.at[(NZ - j) % NZ], p3_ss.at[j], p3_rs.at[(NZ - j) % NZ], dev_z(j)
        )

    def recv_p3(j):
        return remote(rs_c.at[0], rs3.at[j], p3_ss.at[j], p3_rs.at[j], dev_z(j))

    each(NZ, lambda j: copy_p3(j).start())
    rs3[0] = rs_c[z]
    each(NZ, lambda j: recv_p3(j).wait_recv())
    proj[...] = jnp.sum(rs3[...].astype(F32), axis=0).astype(BF16)

    m_copy.wait_send()
    t_copy.wait_send()
    f_copy.wait_send()
    p1.wait_send()
    for k in range(KC):
        each(NZ, lambda j: recv_a(k, j).wait_send())
        each(NP, lambda j: recv_b(k, j).wait_send())
        copy_c(k).wait_send()
        copy_cr(k).wait_send()
    each(NP, lambda j: recv_br(j).wait_send())
    each(NZ, lambda j: recv_ar(j).wait_send())
    each(NP, lambda j: recv_p2(j).wait_send())
    each(NZ, lambda j: recv_p3(j).wait_send())


def moe(rowidx, gate, x, g, mixt, swap, w_in, w_out):
    vmem = pl.BlockSpec(memory_space=pltpu.VMEM)
    hbm = pl.BlockSpec(memory_space=pl.ANY)
    dma = pltpu.SemaphoreType.DMA
    V = pltpu.VMEM
    return pl.pallas_call(
        moe_kernel,
        out_shape=(
            jax.ShapeDtypeStruct((TOK, D), BF16),
            jax.ShapeDtypeStruct((2, TOK, 128), F32),
            jax.ShapeDtypeStruct((D, D), BF16),
            jax.ShapeDtypeStruct((D, D), BF16),
            jax.ShapeDtypeStruct((16, 256), BF16),
        ),
        in_specs=[vmem] * 6 + [hbm] * 2,
        out_specs=(vmem,) * 5,
        scratch_shapes=[
            V((D, D), BF16), V((D, D), BF16),
            V((2, TOK, D), BF16), V((TOK, D), BF16),
            V((2, ALL, TOK), BF16), V((2, ALL, TOK), BF16),
            V((KC, NZ, ROWS, CW), BF16), V((KC, NZ, ROWS, CW), BF16), V((KC, NQ, ROWS, CW), BF16),
            V((2, KC, NP, ROWS, CW), BF16),
            V((4, BLK, D), F32), V((4, BLK, D), F32),
            V((KC, NP * ROWS, CW), BF16), V((KC, NP * ROWS, CW), BF16), V((NP * ROWS, 128), BF16),
            V((4, 4, ROWS, HALF), BF16), V((4, 4, ROWS, HALF), BF16), V((4, BLK, HALF), F32),
            V((NP, ROWS, EXT), BF16), V((NP, ROWS, EXT), BF16),
            V((NQ, ROWS, EXT), BF16), V((NZ, ROWS, EXT), BF16), V((NZ, ROWS, EXT), BF16),
            V((TOK, HALF + 256), F32), V((TOK, HALF + 256), F32),
            V((2, NZ, NQ, 16, 256), BF16), V((2, NZ, NQ, 16, 256), BF16), V((2, NZ, NQ, 16, 256), F32),
            V((2, NZ, NQ, 16, 256), BF16), V((NP, NZ, 16, 256), BF16),
            V((NZ, 16, 256), BF16), V((NZ, 16, 256), BF16),
            dma((2,)), dma, dma, dma, dma,
            dma((KC, NZ)), dma((KC, NZ)), dma((KC, NP)), dma((KC, NP)), dma((KC,)), dma((KC,)),
            dma((4,)), dma((4,)), dma((NP,)), dma((NP,)), dma((NZ,)), dma((NZ,)), dma, dma, dma, dma,
            dma((NP,)), dma((NP,)), dma((NZ,)), dma((NZ,)),
        ],
        compiler_params=pltpu.CompilerParams(
            collective_id=0, has_side_effects=True, vmem_limit_bytes=62 * 1024 * 1024
        ),
        cost_estimate=pl.CostEstimate(flops=14_000_000_000, bytes_accessed=12_000_000, transcendentals=1_310_720),
    )(rowidx, gate, x, g, mixt, swap, w_in, w_out)


def attention_forward(queries, key_rows, value_head_rows, length):
    heads = queries.shape[1] // HEAD_SIZE
    scale = 1.0 / math.sqrt(HEAD_SIZE)
    spec = (queries.shape[0], heads, HEAD_SIZE)
    scores = jnp.einsum(
        "fcy,wcy->cfw", queries.reshape(spec), key_rows.reshape(spec), preferred_element_type=F32
    ) * scale
    live = jnp.arange(queries.shape[0], dtype=jnp.int32) < length
    scores = jnp.where(live[None, None, :], scores, -1000000000.0)
    top = jnp.max(scores, axis=-1, keepdims=True)
    expo = jnp.exp(scores - top)
    probs = expo / jnp.sum(expo, axis=-1, keepdims=True)
    mixt = jnp.einsum(
        "fwn,nfy->fyw", probs.astype(BF16), value_head_rows.reshape(spec), preferred_element_type=F32
    ).astype(BF16)
    return probs, mixt.reshape(queries.shape[1], queries.shape[0])


def attention_backward(queries, key_rows, value_head_rows, d_heads, probs):
    heads = queries.shape[1] // HEAD_SIZE
    scale = 1.0 / math.sqrt(HEAD_SIZE)
    spec = (queries.shape[0], heads, HEAD_SIZE)
    qmat, kmat, vmat, gmat = (a.reshape(spec) for a in (queries, key_rows, value_head_rows, d_heads))
    d_probs = jnp.einsum("fcy,wcy->cfw", gmat, vmat, preferred_element_type=F32)
    grad_v = jnp.einsum("hqk,qhd->khd", probs.astype(BF16), gmat, preferred_element_type=F32).astype(BF16)
    inner = jnp.sum(d_probs * probs, axis=-1, keepdims=True)
    dscore = (probs * (d_probs - inner)).astype(BF16)
    grad_q = (jnp.einsum("fwn,nfy->wfy", dscore, kmat, preferred_element_type=F32) * scale).astype(BF16)
    grad_k = (jnp.einsum("hqk,qhd->khd", dscore, qmat, preferred_element_type=F32) * scale).astype(BF16)
    return grad_q.reshape(queries.shape), grad_k.reshape(queries.shape), grad_v.reshape(queries.shape)


def on_device(
    mid_acts, out_grad, queries, key_rows, value_head_rows, seq_lengths,
    expert_ids, gate_probs, wide_in, wide_out, attn_proj,
):
    experts = lax.axis_size("expert")
    slots = group_slots(expert_ids, experts, CAP)
    ids = expert_ids.T
    z = lax.axis_index("expert") // NQ
    core = lax.axis_index("replica") % 2
    place = ((ids // NQ + NZ - z) % NZ) * ROWS + core * (NQ * CAP) + (ids % NQ) * CAP + slots
    rowidx = jnp.where(slots >= 0, place, -1).astype(jnp.int32)
    gate_t = gate_probs.T.astype(F32)
    probs, mixt = attention_forward(queries, key_rows, value_head_rows, seq_lengths[0])
    grad_mid, gates, grad_in, grad_out, proj = moe(
        rowidx, gate_t, mid_acts, out_grad, mixt, jnp.asarray(swap_table(), BF16), wide_in[0], wide_out[0]
    )
    grad_gates = (jnp.sum(gates, axis=2) / gate_t).T
    d_heads = dot_nt(grad_mid, attn_proj).astype(BF16)
    grad_q, grad_k, grad_v = attention_backward(queries, key_rows, value_head_rows, d_heads, probs)
    return (grad_mid, grad_q, grad_k, grad_v, grad_gates, grad_in[None], grad_out[None], proj)


def solution(mesh):
    both = ("expert", "replica")
    return jax.shard_map(
        on_device,
        mesh=mesh,
        in_specs=(
            P(both, None), P(both, None), P(both, None), P(both, None), P(both, None), P(both),
            P(both, None), P(both, None), P("expert", None, "replica"), P("expert", "replica", None), P(),
        ),
        out_specs=(
            P(both, None), P(both, None), P(both, None), P(both, None), P(both, None),
            P("expert", None, "replica"), P("expert", "replica", None), P("expert", "replica"),
        ),
        check_vma=False,
    )
```

time: 674 us -> 175 us (0.26); the launches traced: 666 us -> 174 us
  waiting for transfers between devices: 400 us -> 0 us
  Pallas kernels: 0 us -> 150 us
  blocking collectives: 98.9 us -> 0 us
  matrix products: 60.6 us -> 7.04 us
  local copies, waits for them, and re-layouts: 58.8 us -> 12 us
  starting transfers between devices: 24.4 us -> 0 us
  between operations: 15.6 us -> 1.46 us
    reduce_scatter x4 -> x0, waiting for transfers between devices: 335 us -> none  [the longest x1 260 us: on_device(): lax.psum_scatter(proj_term, 'expert', scatter_dimension=0, tiled=True)]
    pallas_call x0 -> x1, Pallas kernels: none -> 150 us  [moe(): pl.pallas_call(moe_kernel, out_shape=(jax.ShapeDtypeStruct((TOK, D), BF16...]
    all_to_all x3 -> x0, blocking collectives: 91.1 us -> none  [the longest x1 40.7 us: on_device(): lax.all_to_all(slot_x, 'expert', split_axis=0, concat_axis=0, tiled=True)]
    all_to_all x2 -> x0, waiting for transfers between devices: 65.2 us -> none  [the longest x1 46.2 us: on_device(): lax.all_to_all(back_dx, 'expert', split_axis=0, concat_axis=0, tiled=True)]
    dot_general x18 -> x6, matrix products: 59 us -> 6.51 us  [the longest x1 2.52 us: dot_nt(): lax.dot_general(a, b, (((1,), (1,)), ((), ())), preferred_element_type=F32)]
    convert_element_type x7 -> x1, local copies, waits for them, and re-layouts: 25.7 us -> 0.17 us  [on_device(): d_heads = dot_nt(grad_mid, attn_proj).astype(BF16)]
    all_to_all x2 -> x0, starting transfers between devices: 24 us -> none  [the longest x1 12.2 us: on_device(): lax.all_to_all(back_dx, 'expert', split_axis=0, concat_axis=0, tiled=True)]
    reshape x7 -> x0, local copies, waits for them, and re-layouts: 14.5 us -> none  [the longest x1 6.23 us: on_device(): all_x.reshape(-1, width)]
  transfers between devices with their start and end apart: 8 -> 0, of which waited for: 6 -> 0; matrix products, arithmetic and copies ran while one was open for 13% -> 0% of each run, Pallas kernels for 0% -> 0%
where the time goes in v1:
time: 175 us; the launch traced here: 174 us
  Pallas kernels  150 us (86%)
  local copies, waits for them, and re-layouts  12 us (7%)
  matrix products  7.04 us (4%)
  other arithmetic  3.51 us (2%)
    pallas_call x1, Pallas kernels, moe(): pl.pallas_call(moe_kernel, out_shape=(jax.ShapeDtypeStruct((TOK, D), BF16...  150 us
    unnamed x28, local copies, waits for them, and re-layouts  10.9 us

profile of v1, /device:TPU:4, one launch (start us, length us, event | category | flops | bytes accessed | tf_op | source)
XLA Modules:
  0.0 173.9 jit_solution(5252732355303339005)
XLA Ops:
  0.7 0.8 slice_bitcast_fusion.1
  1.5 0.6 reduce-window.6
  2.1 0.2 slice_reduce_fusion
  2.3 0.1 fusion.10
  2.4 1.3 compare_select_fusion.3.rowidx
  3.7 1.1 copy.36
  4.8 1.1 copy.37
  6.6 0.5 fusion.22
  7.1 0.2 copy.38
  7.3 0.0 copy-start.4
  7.3 0.0 copy-start.8
  7.3 1.4 convolution_convert_fusion
  8.8 0.6 convert_bitcast_fusion.gate
  9.3 149.9 %shard_map.179 = (bf16[128,1024]{1,0:T(8,128)(2,1)}, f32[2,128,128]{2,1,0:T(8,128)}, bf16[1024,1024]{1,0:T(8,128)(2,1)}, bf16[1024,1024]{1,0:T(8,128)(2,1)}, bf16[16,256]{1,0:T(8,128)(2,1)}) custom-call(s32[2,128]{1,0:T(2,128)} %compare_select_fusion.3.rowidx, f32[2,128]{1,0:T(2,128)} %convert_bitcast_fusion.gate, bf16[128,1024]{1,0:T(8,128)(2,1)} %x_ref.1, ...), custom_call_target="tpu_custom_call" | custom-call | flops 14000000000 | bytes 12000000 | tf_op jit(solution)/shard_map/pallas_call | solution.py:414
  159.2 2.5 %convolution_convert_fusion.2 = bf16[128,1024]{1,0:T(8,128)(2,1)S(1)} fusion(bf16[128,1024]{1,0:T(8,128)(2,1)} %get-tuple-element.50, bf16[1024,1024]{1,0:T(8,128)(2,1)} %param.22), kind=kOutput, calls=%fused_computation.11 | convolution fusion | flops 268566528 | bytes 2621440 | tf_op jit(solution)/shard_map/dot_general | solution.py:45
  161.7 0.2 copy.40
  161.9 0.0 copy-start.5
  161.9 0.8 convolution_convert_fusion.1
  162.7 0.9 copy.46
  163.6 0.4 multiply_reduce_fusion
  163.9 0.2 multiply_convert_fusion
  164.2 1.2 fusion.4
  165.3 1.8 %copy.45 = bf16[128,1024]{1,0:T(8,128)(2,1)} copy(bf16[128,1024]{0,1:T(8,128)(2,1)} %bitcast.94) | data formatting | bytes 524288
  167.1 0.3 fusion.5
  167.4 0.9 copy.44
  168.3 0.1 reduce_sum.44
  168.4 0.6 convert_divide_fusion
  168.9 0.7 copy.58
  169.7 1.3 copy.59
  171.0 1.0 copy-done
  172.0 1.3 copy.60
  173.3 0.6 copy.61
  (19 shorter events, 0.1 us)
Async XLA Ops:
  0.6 6.5 %copy-start.3 = (bf16[128,1024]{1,0:T(8,128)(2,1)S(1)}, bf16[128,1024]{1,0:T(8,128)(2,1)}, u32[]{:S(2)}) copy-start(bf16[128,1024]{1,0:T(8,128)(2,1)} %param.16) | copy-start | bytes 786436
  7.3 1.4 copy-start.4
  7.3 1.4 copy-start.8
  161.9 1.6 copy-start.5
  164.1 4.1 %copy-start.6 = (f32[2,128,128]{2,1,0:T(8,128)S(1)}, f32[2,128,128]{2,1,0:T(8,128)}, u32[]{:S(2)}) copy-start(f32[2,128,128]{2,1,0:T(8,128)} %get-tuple-element.14) | copy-start | bytes 393220
  164.2 4.8 %copy-start.2 = (bf16[128,1024]{1,0:T(8,128)(2,1)S(1)}, bf16[128,1024]{1,0:T(8,128)(2,1)}, u32[]{:S(2)}) copy-start(bf16[128,1024]{1,0:T(8,128)(2,1)} %get-tuple-element.50) | copy-start | bytes 786436
  164.2 5.5 %copy-start.1 = (bf16[1024,1024]{1,0:T(8,128)(2,1)S(1)}, bf16[1024,1024]{1,0:T(8,128)(2,1)}, u32[]{:S(2)}) copy-start(bf16[1024,1024]{1,0:T(8,128)(2,1)} %get-tuple-element.15) | copy-start | bytes 6291460
  169.7 2.3 %copy-start = (bf16[1024,1024]{1,0:T(8,128)(2,1)S(1)}, bf16[1024,1024]{1,0:T(8,128)(2,1)}, u32[]{:S(2)}) copy-start(bf16[1024,1024]{1,0:T(8,128)(2,1)} %get-tuple-element.16) | copy-start | bytes 6291460
  172.0 1.3 copy-start.7

commit v2 on v1

v2 whole, which is shorter than its diff:
```python
import math

import jax
import jax.numpy as jnp
from jax import lax
from jax.experimental import pallas as pl
from jax.experimental.pallas import tpu as pltpu
from jax.sharding import PartitionSpec as P

HEAD_SIZE = 64
GELU_C = 0.7978845608028654
GELU_A = 0.044715
MESH = pl.DeviceIdType.MESH

NZ, NQ, NP = 8, 8, 16
CAP = 5
TOK = 128
D = 1024
ROWS = 2 * NQ * CAP
ALL = NZ * ROWS
KC, CW = 4, 256
BLK = 4 * ROWS
F32 = jnp.float32
BF16 = jnp.bfloat16


def dot_nn(a, b):
    return jnp.dot(a, b, preferred_element_type=F32)


def dot_nt(a, b):
    return lax.dot_general(a, b, (((1,), (1,)), ((), ())), preferred_element_type=F32)


def dot_tn(a, b):
    return lax.dot_general(a, b, (((0,), (0,)), ((), ())), preferred_element_type=F32)


def moe_kernel(
    length, ids_ref, gate_ref, x_hbm, g_hbm, q_hbm, k_hbm, v_hbm, ap_hbm, w_in_hbm, w_out_hbm,
    mid, grad_q, grad_k, grad_v, gates, gin_hbm, gout_hbm, proj,
    q_buf, k_buf, v_buf, ap, probs, d_heads,
    w_in, w_arr, w_out, swap, mixt, grad_in, grad_out, xg, t_buf, t_use, t_all, t_one, sa, ra, sb, rr,
    pre, dact, act, dpre, side, ds, dr, do, sbr, rbr, yy, sar, rar,
    sp, sp_in, ys, sz, sz_in, ga, ga_in, mo, mo_in, rs_b, rs2, rs_c, rs3,
    w_sem, n_sem, o_sem, pair_ss, pair_rs, a_ss, a_rs, b_ss, b_rs, c_ss, c_rs, cr_ss, cr_rs,
    br_ss, br_rs, ar_ss, ar_rs, sp_ss, sp_rs, sz_ss, sz_rs, p2_ss, p2_rs, p3_ss, p3_rs,
):
    e = lax.axis_index("expert")
    r = lax.axis_index("replica")
    z, q, xh, c = e // NQ, e % NQ, r // 2, r % 2
    pm = xh * NQ + q
    other = 1 - c
    partner = (e, xh * 2 + other)
    late = []

    def dev_z(j):
        return (((z + j) % NZ) * NQ + q, r)

    def plane_of(j):
        return (pm + j) % NP

    def dev_p(j):
        p = plane_of(j)
        return (z * NQ + p % NQ, (p // NQ) * 2 + c)

    def remote(src, dst, ss, rs, dev):
        return pltpu.make_async_remote_copy(
            src_ref=src, dst_ref=dst, send_sem=ss, recv_sem=rs, device_id=dev, device_id_type=MESH
        )

    def pair(n, src, dst):
        return remote(src, dst, pair_ss.at[n], pair_rs.at[n], partner)

    def each(count, body):
        def step(j, _):
            body(j)
            return 0

        lax.fori_loop(1, count, step, 0)

    def piece(xhi, core, h):
        return pl.ds(pl.multiple_of(xhi * 512 + core * 256 + h * 128, 128), 128)

    tokens = [
        pltpu.make_async_copy(x_hbm, xg.at[0, c], w_sem.at[3]),
        pltpu.make_async_copy(g_hbm, xg.at[1, c], w_sem.at[4]),
    ]
    heads_in = [
        pltpu.make_async_copy(q_hbm, q_buf, w_sem.at[5]),
        pltpu.make_async_copy(k_hbm, k_buf, w_sem.at[6]),
        pltpu.make_async_copy(v_hbm, v_buf, w_sem.at[7]),
    ]
    loads = [
        pltpu.make_async_copy(w_in_hbm, w_in, w_sem.at[1]),
        pltpu.make_async_copy(w_out_hbm, w_out, w_sem.at[2]),
        pltpu.make_async_copy(ap_hbm, ap, w_sem.at[0]),
    ]
    arranged = []
    for n in range(8):
        core, h, xhi = n // 4, (n // 2) % 2, n % 2
        arranged.append(
            pltpu.make_async_copy(
                w_in_hbm.at[pl.ds(xhi * 512 + core * 256 + h * 128, 128)],
                w_arr.at[core, h, pl.ds(xhi * 128, 128)],
                n_sem.at[n],
            )
        )
    for copy in tokens + heads_in + loads + arranged:
        copy.start()

    bar = pltpu.get_barrier_semaphore()
    pl.semaphore_signal(bar, inc=1, device_id=partner, device_id_type=MESH)
    each(NZ, lambda j: pl.semaphore_signal(bar, inc=1, device_id=dev_z(j), device_id_type=MESH))
    each(NP, lambda j: pl.semaphore_signal(bar, inc=1, device_id=dev_p(j), device_id_type=MESH))

    above = lax.broadcasted_iota(jnp.int32, (TOK, TOK), 0)
    along = lax.broadcasted_iota(jnp.int32, (TOK, TOK), 1)

    def to_column(row):
        return jnp.sum(jnp.where(above == along, jnp.broadcast_to(row, (TOK, TOK)), 0), axis=1, keepdims=True)

    def count(which):
        return jnp.sum(jnp.where(which, 1, 0), axis=0, keepdims=True)

    ids = [ids_ref[k : k + 1, :] for k in range(2)]
    columns = [to_column(row) for row in ids]
    gate = [gate_ref[k : k + 1, :].astype(F32) for k in range(2)]
    slot = [
        count((columns[0] == ids[0]) & (above < along)),
        count(columns[0] == ids[1]) + count((columns[1] == ids[1]) & (above < along)),
    ]
    rows_of = lax.broadcasted_iota(jnp.int32, (ALL, TOK), 0)
    signed = None
    for k in range(2):
        place = ((ids[k] // NQ + NZ - z) % NZ) * ROWS + c * (NQ * CAP) + (ids[k] % NQ) * CAP + slot[k]
        place = jnp.where(slot[k] < CAP, place, -1)
        term = jnp.where(rows_of == place, gate[k] if k == 0 else -gate[k], 0.0)
        signed = term if signed is None else signed + term
    t_buf[c] = signed.astype(BF16)
    for copy in tokens:
        copy.wait()
    pl.semaphore_wait(bar, NZ + NP - 1)

    t_copy = pair(0, t_buf.at[c], t_buf.at[c])
    m_copy = pair(1, xg.at[other, c], xg.at[other, c])
    n_copy = pair(2, xg.at[c, c], xg.at[c, c])
    t_copy.start()
    m_copy.start()
    n_copy.start()
    late.extend([t_copy.wait_send, m_copy.wait_send, n_copy.wait_send])
    t_copy.wait_recv()
    for j in range(2):
        size = jnp.abs(t_buf[j].astype(F32))
        t_use[j] = jnp.where(c == 0, jnp.where(size > 0.0, 1.0, 0.0), size).astype(BF16)
    pair(1, xg.at[c, other], xg.at[c, other]).wait_recv()

    def copy_a(k, j):
        return remote(sa.at[k, j], ra.at[k, (NZ - j) % NZ], a_ss.at[k, j], a_rs.at[k, (NZ - j) % NZ], dev_z(j))

    def recv_a(k, j):
        return remote(sa.at[k, j], ra.at[k, j], a_ss.at[k, j], a_rs.at[k, j], dev_z(j))

    def copy_b(k, j):
        return remote(
            sb.at[k, plane_of(j) % NQ], rr.at[c, k, (NP - j) % NP], b_ss.at[k, j], b_rs.at[k, (NP - j) % NP], dev_p(j)
        )

    def recv_b(k, j):
        return remote(sb.at[k, 0], rr.at[c, k, j], b_ss.at[k, j], b_rs.at[k, j], dev_p(j))

    def copy_c(k):
        return remote(rr.at[c, k], rr.at[c, k], c_ss.at[k], c_rs.at[k], partner)

    def recv_c(k):
        return remote(rr.at[other, k], rr.at[other, k], c_ss.at[k], c_rs.at[k], partner)

    def stage_a(k):
        each(NZ, lambda j: copy_a(k, j).start())
        ra[k, 0] = sa[k, 0]

    AHEAD = 2
    for k in range(KC):
        cols = slice(k * CW, (k + 1) * CW)
        rows = dot_nn(t_use[0], xg[c, 0, :, cols]) + dot_nn(t_use[1], xg[c, 1, :, cols])
        sa[k] = rows.astype(BF16).reshape(NZ, ROWS, CW)
        if k < AHEAD:
            stage_a(k)
    left_lane = lax.broadcasted_iota(jnp.int32, (TOK, 128), 1) < HEAD_SIZE
    live = lax.broadcasted_iota(jnp.int32, (TOK, TOK), 1) < length[0]
    SCALE = 1.0 / math.sqrt(HEAD_SIZE)

    def masked(block, n):
        block = block.astype(F32)
        return (jnp.where(left_lane, block, 0.0) if n == 0 else jnp.where(left_lane, 0.0, block)).astype(BF16)

    def forward(p, _):
        at = pl.ds(pl.multiple_of(p * 128, 128), 128)
        qp, kp, vp = q_buf[:, at], k_buf[:, at], v_buf[:, at]
        out = []
        for n in range(2):
            scores = jnp.where(live, dot_nt(masked(qp, n), kp) * SCALE, -1000000000.0)
            expo = jnp.exp(scores - jnp.max(scores, axis=1, keepdims=True))
            prob = expo / jnp.sum(expo, axis=1, keepdims=True)
            probs[2 * p + n] = prob
            out.append(dot_nn(prob.astype(BF16), vp))
        mixt[c, at, :] = jnp.where(left_lane, out[0], out[1]).T.astype(BF16)
        return 0

    for copy in heads_in:
        copy.wait()
    lax.fori_loop(0, 8, forward, 0)

    row = lax.broadcasted_iota(jnp.int32, (8, ALL), 1)
    place = (row % (NQ * CAP)) // CAP * ROWS + (row % ROWS) // (NQ * CAP) * (NQ * CAP) + row // ROWS * CAP + row % CAP
    for n in range(8):
        rows = lax.broadcasted_iota(jnp.int32, (ROWS, ALL), 0) + n * ROWS
        swap[n * ROWS : (n + 1) * ROWS, :] = jnp.where(rows == place[0:1, :], 1.0, 0.0).astype(BF16)
    x_copy = pair(3, mixt.at[c], mixt.at[c])
    x_copy.start()
    late.append(x_copy.wait_send)

    def stage_b(k):
        each(NZ, lambda j: recv_a(k, j).wait_recv())
        if k + AHEAD < KC:
            stage_a(k + AHEAD)
        rows = dot_nn(swap[...], ra[k].reshape(ALL, CW))
        sb[k] = rows.astype(BF16).reshape(NQ, ROWS, CW)
        each(NP, lambda j: copy_b(k, j).start())
        rr[c, k, 0] = sb[k, q]

    def stage_c(k):
        each(NP, lambda j: recv_b(k, j).wait_recv())
        copy_c(k).start()

    def stage_d(k):
        recv_c(k).wait_recv()
        if k == 0:
            loads[0].wait()
            loads[1].wait()

        def body(i, _):
            xk = rr[0, k, pl.ds(4 * i, 4)].reshape(BLK, CW)
            gk = rr[1, k, pl.ds(4 * i, 4)].reshape(BLK, CW)
            p_new = dot_nn(xk, w_in[k * CW : (k + 1) * CW, :])
            d_new = dot_nt(gk, w_out[:, k * CW : (k + 1) * CW])
            if k == 0:
                pre[i] = p_new
                dact[i] = d_new
            else:
                pre[i] += p_new
                dact[i] += d_new
            return 0

        lax.fori_loop(0, 4, body, 0)

    for step in range(KC + 2):
        if step < KC:
            stage_b(step)
        if 0 <= step - 1 < KC:
            stage_c(step - 1)
        if 0 <= step - 2 < KC:
            stage_d(step - 2)
        if step == 1:
            loads[2].wait()
            for copy in arranged:
                copy.wait()
    for k in range(KC):
        late.append(lambda k=k: each(NZ, lambda j: recv_a(k, j).wait_send()))
        late.append(lambda k=k: each(NP, lambda j: recv_b(k, j).wait_send()))
        late.append(copy_c(k).wait_send)

    SUB = 32

    def gelu_block(i):
        def body(n, _):
            at = pl.multiple_of(n * SUB, SUB)
            u = pre[i, pl.ds(at, SUB), :]
            da = dact[i, pl.ds(at, SUB), :]
            uu = u * u
            inner = jnp.tanh(GELU_C * (u + GELU_A * uu * u))
            half = 0.5 * (1.0 + inner)
            a = (u * half).astype(BF16)
            slope = half + 0.5 * u * (1.0 - inner * inner) * (GELU_C + (3.0 * GELU_A * GELU_C) * uu)
            dp = (da * slope).astype(BF16)
            s = jnp.sum(a.astype(F32) * da, axis=1, keepdims=True)
            to = pl.multiple_of(i * BLK + at, SUB)
            side[pl.ds(to, SUB), :] = jnp.broadcast_to(s, (SUB, 128))
            for f in range(KC):
                act[f, pl.ds(to, SUB), :] = a[:, f * CW : (f + 1) * CW]
                dpre[f, pl.ds(to, SUB), :] = dp[:, f * CW : (f + 1) * CW]
            return 0

        lax.fori_loop(0, BLK // SUB, body, 0)

    def copy_cr(i):
        return remote(ds.at[i], dr.at[i], cr_ss.at[i], cr_rs.at[i], partner)

    def dx_block(i):
        def part(core, h):
            total = None
            for f in range(KC):
                term = dot_nt(dpre[f, i * BLK : (i + 1) * BLK, :], w_arr[core, h, :, f * CW : (f + 1) * CW])
                total = term if total is None else total + term
            return total

        for h in range(2):
            ds[i, h] = part(other, h).astype(BF16).reshape(4, ROWS, CW)
        copy_cr(i).start()
        late.append(copy_cr(i).wait_send)
        for h in range(2):
            do[i, h] = part(c, h)

    def copy_br(h, j):
        return remote(sbr.at[h, j], rbr.at[h, (NP - j) % NP], br_ss.at[h, j], br_rs.at[h, (NP - j) % NP], dev_p(j))

    def recv_br(h, j):
        return remote(sbr.at[h, j], rbr.at[h, j], br_ss.at[h, j], br_rs.at[h, j], dev_p(j))

    def copy_sp(j):
        return remote(sp.at[j], sp_in.at[(NP - j) % NP], sp_ss.at[j], sp_rs.at[(NP - j) % NP], dev_p(j))

    def recv_sp(j):
        return remote(sp.at[j], sp_in.at[j], sp_ss.at[j], sp_rs.at[j], dev_p(j))

    diagonal = lax.broadcasted_iota(jnp.int32, (ROWS, 128), 0) == lax.broadcasted_iota(jnp.int32, (ROWS, 128), 1)

    def return_block(i, h):
        if h == 0:
            copy_cr(i).wait_recv()
        for n in range(4):
            p = 4 * i + n
            sbr[h, p] = (do[i, h, n * ROWS : (n + 1) * ROWS, :] + dr[i, h, n].astype(F32)).astype(BF16)
            if p:
                copy_br(h, p).start()

    def side_block(i):
        for n in range(4):
            p = 4 * i + n
            row = jnp.sum(jnp.where(diagonal, side[p * ROWS : (p + 1) * ROWS, :], 0.0), axis=0, keepdims=True)
            sp[p] = jnp.broadcast_to(row, (8, 128))
            if p:
                copy_sp(p).start()

    for i in range(5):
        if i < 4:
            gelu_block(i)
            dx_block(i)
        if i > 0:
            return_block(i - 1, 0)
    for i in range(4):
        return_block(i, 1)
    for i in range(4):
        side_block(i)
    for h in range(2):
        late.append(lambda h=h: each(NP, lambda j: recv_br(h, j).wait_send()))
    late.append(lambda: each(NP, lambda j: recv_sp(j).wait_send()))

    def wide_in_body(n, _):
        at = pl.multiple_of((n // KC) * CW, CW)
        f = n % KC
        rows = rr[0, n // KC].reshape(NP * ROWS, CW)
        term = dot_tn(rows, dpre[f]).astype(BF16)
        grad_in[pl.ds(at, CW), pl.ds(pl.multiple_of(f * CW, CW), CW)] = term
        return 0

    def wide_out_body(n, _):
        f = n // KC
        k = n % KC
        rows = rr[1, k].reshape(NP * ROWS, CW)
        term = dot_tn(act[f], rows).astype(BF16)
        grad_out[pl.ds(pl.multiple_of(f * CW, CW), CW), pl.ds(pl.multiple_of(k * CW, CW), CW)] = term
        return 0

    lax.fori_loop(0, KC * KC, wide_in_body, 0)
    out_in = pltpu.make_async_copy(grad_in, gin_hbm, o_sem.at[0])
    out_in.start()
    late.append(out_in.wait)

    for j in range(2):
        t = t_buf[j].astype(F32)
        t_all[j] = jnp.where(t != 0.0, 1.0, 0.0).T.astype(BF16)
        t_one[j, 0] = jnp.where(t > 0.0, 1.0, 0.0).astype(BF16)
        t_one[j, 1] = jnp.where(t < 0.0, 1.0, 0.0).astype(BF16)

    def copy_ar(h, j):
        return remote(sar.at[h, j], rar.at[h, (NZ - j) % NZ], ar_ss.at[h, j], ar_rs.at[h, (NZ - j) % NZ], dev_z(j))

    def recv_ar(h, j):
        return remote(sar.at[h, j], rar.at[h, j], ar_ss.at[h, j], ar_rs.at[h, j], dev_z(j))

    def copy_sz(j):
        return remote(sz.at[j], sz_in.at[(NZ - j) % NZ], sz_ss.at[j], sz_rs.at[(NZ - j) % NZ], dev_z(j))

    def recv_sz(j):
        return remote(sz.at[j], sz_in.at[j], sz_ss.at[j], sz_rs.at[j], dev_z(j))

    def stage_z(h):
        each(NP, lambda j: recv_br(h, j).wait_recv())
        for j in range(NQ):
            one = sbr if j == 0 else rbr
            yy[(q + j) % NQ] = (one[h, j].astype(F32) + rbr[h, j + NQ].astype(F32)).astype(BF16)
        sar[h] = dot_nn(swap[...], yy[...].reshape(ALL, CW)).astype(BF16).reshape(NZ, ROWS, CW)
        each(NZ, lambda j: copy_ar(h, j).start())
        rar[h, 0] = sar[h, 0]
        late.append(lambda: each(NZ, lambda j: recv_ar(h, j).wait_send()))

    lanes = lax.broadcasted_iota(jnp.int32, (ROWS, 128), 1)

    def side_z():
        each(NP, lambda j: recv_sp(j).wait_recv())
        for j in range(NQ):
            one = sp if j == 0 else sp_in
            row = (one[j] + sp_in[j + NQ])[0:1, :]
            s = jnp.sum(jnp.where(diagonal, jnp.broadcast_to(row, (ROWS, 128)), 0.0), axis=1, keepdims=True)
            hi = s.astype(BF16).astype(F32)
            ys[(q + j) % NQ] = jnp.where(lanes == 0, hi, jnp.where(lanes == 1, s - hi, 0.0)).astype(BF16)
        back = dot_nn(swap[...], ys[...].reshape(ALL, 128))
        for n in range(NZ):
            s = jnp.sum(back[n * ROWS : (n + 1) * ROWS, :], axis=1, keepdims=True)
            row = jnp.sum(jnp.where(diagonal, s, 0.0), axis=0, keepdims=True)
            sz[n] = jnp.broadcast_to(row, (8, 128))
        each(NZ, lambda j: copy_sz(j).start())
        sz_in[0] = sz[0]
        late.append(lambda: each(NZ, lambda j: recv_sz(j).wait_send()))

    stage_z(0)
    lax.fori_loop(0, KC * KC // 2, wide_out_body, 0)
    stage_z(1)
    side_z()
    lax.fori_loop(KC * KC // 2, KC * KC, wide_out_body, 0)
    out_out = pltpu.make_async_copy(grad_out, gout_hbm, o_sem.at[1])
    out_out.start()
    late.append(out_out.wait)
    pair(2, xg.at[other, other], xg.at[other, other]).wait_recv()
    pair(3, mixt.at[other], mixt.at[other]).wait_recv()

    def copy_p2(h, j):
        p = plane_of(j)
        return remote(
            rs_b.at[h, p // NQ, :, p % NQ], rs2.at[h, (NP - j) % NP], p2_ss.at[h, j], p2_rs.at[h, (NP - j) % NP],
            dev_p(j),
        )

    def recv_p2(h, j):
        return remote(rs_b.at[h, 0, :, 0], rs2.at[h, j], p2_ss.at[h, j], p2_rs.at[h, j], dev_p(j))

    def mo_copy(h):
        return pair(4 + h, mo.at[h], mo_in.at[h])

    def home(h):
        each(NZ, lambda j: recv_ar(h, j).wait_recv())
        rows = rar[h].reshape(ALL, CW)
        theirs = dot_nn(t_all[other], rows)
        ours = dot_nn(t_all[c], rows)
        mine = []
        for xhi in range(2):
            lane = slice(xhi * 128, (xhi + 1) * 128)
            mo[h, :, lane] = (xg[1, other, :, piece(xhi, c, h)].astype(F32) + theirs[:, lane]).astype(BF16)
            own = (xg[1, c, :, piece(xhi, c, h)].astype(F32) + ours[:, lane]).astype(BF16)
            mid[:, piece(xhi, c, h)] = own
            mine.append(own)
        mo_copy(h).start()
        late.append(mo_copy(h).wait_send)
        for xhi in range(2):
            lane = slice(xhi * 128, (xhi + 1) * 128)
            part = dot_nn(mixt[c], mine[xhi]) + dot_nn(mixt[other], mo[h, :, lane])
            rs_b[h, xhi] = part.astype(BF16).reshape(NZ, NQ, 16, 128)
        each(NP, lambda j: copy_p2(h, j).start())
        rs2[h, 0] = rs_b[h, xh, :, q]
        late.append(lambda: each(NP, lambda j: recv_p2(h, j).wait_send()))

    home(0)
    home(1)

    for h in range(2):
        mo_copy(h).wait_recv()
        for xhi in range(2):
            mid[:, piece(xhi, other, h)] = mo_in[h, :, xhi * 128 : (xhi + 1) * 128]

    for n in range(4):
        rows = slice(n * CW, (n + 1) * CW)
        d_heads[:, rows] = dot_nt(mid[...], ap[rows, :]).astype(BF16)

    def backward(p, _):
        at = pl.ds(pl.multiple_of(p * 128, 128), 128)
        qp, kp, vp, gp = q_buf[:, at], k_buf[:, at], v_buf[:, at], d_heads[:, at]
        gq, gk, gv = [], [], []
        for n in range(2):
            prob = probs[2 * p + n]
            gv.append(dot_tn(prob.astype(BF16), gp))
            d_prob = dot_nt(masked(gp, n), vp)
            inner = jnp.sum(d_prob * prob, axis=1, keepdims=True)
            d_score = (prob * (d_prob - inner)).astype(BF16)
            gq.append(dot_nn(d_score, kp))
            gk.append(dot_tn(d_score, qp))
        grad_v[:, at] = jnp.where(left_lane, gv[0], gv[1]).astype(BF16)
        grad_q[:, at] = (jnp.where(left_lane, gq[0], gq[1]) * SCALE).astype(BF16)
        grad_k[:, at] = (jnp.where(left_lane, gk[0], gk[1]) * SCALE).astype(BF16)
        return 0

    lax.fori_loop(0, 4, backward, 0)

    for h in range(2):
        each(NP, lambda j: recv_p2(h, j).wait_recv())
        total = lax.fori_loop(1, NP, lambda j, t: t + rs2[h, j].astype(F32), rs2[h, 0].astype(F32))
        rs_c[:, :, h * 128 : (h + 1) * 128] = total.astype(BF16)

    def copy_p3(j):
        return remote(
            rs_c.at[(z + j) % NZ], rs3.at[(NZ - j) % NZ], p3_ss.at[j], p3_rs.at[(NZ - j) % NZ], dev_z(j)
        )

    def recv_p3(j):
        return remote(rs_c.at[0], rs3.at[j], p3_ss.at[j], p3_rs.at[j], dev_z(j))

    each(NZ, lambda j: copy_p3(j).start())
    rs3[0] = rs_c[z]
    late.append(lambda: each(NZ, lambda j: recv_p3(j).wait_send()))

    each(NZ, lambda j: recv_sz(j).wait_recv())
    row16 = lax.broadcasted_iota(jnp.int32, (16, 128), 0)

    def gate_terms(j):
        out = []
        for k in range(2):
            total = None
            for n in range(NZ):
                row = sz_in[n][0:1, :]
                hi = row.astype(BF16).astype(F32)
                both = jnp.where(row16 == 0, hi, jnp.where(row16 == 1, row - hi, 0.0)).astype(BF16)
                term = dot_nn(both[:, 0:ROWS], t_one[j, k, n * ROWS : (n + 1) * ROWS, :])
                total = term if total is None else total + term
            out.append(jnp.sum(total, axis=0, keepdims=True))
        return jnp.concatenate(out + [jnp.zeros((6, 128), F32)], axis=0)

    ga[...] = gate_terms(other)
    ga_copy = pair(6, ga, ga_in)
    ga_copy.start()
    late.append(ga_copy.wait_send)
    ours = gate_terms(c)
    lax.fori_loop(4, 8, backward, 0)
    ga_copy.wait_recv()
    for k in range(2):
        gates[k : k + 1, :] = (ours[k : k + 1, :] + ga_in[k : k + 1, :]) / gate[k]

    each(NZ, lambda j: recv_p3(j).wait_recv())
    proj[...] = jnp.sum(rs3[...].astype(F32), axis=0).astype(BF16)

    for wait in late:
        wait()


def moe(lengths, ids, gate, x, g, q, k, v, ap, w_in, w_out):
    vmem = pl.BlockSpec(memory_space=pltpu.VMEM)
    smem = pl.BlockSpec(memory_space=pltpu.SMEM)
    hbm = pl.BlockSpec(memory_space=pl.ANY)
    V = pltpu.VMEM

    def dma(*shape):
        return [pltpu.SemaphoreType.DMA(shape)] * 2

    return pl.pallas_call(
        moe_kernel,
        out_shape=(
            *[jax.ShapeDtypeStruct((TOK, D), BF16)] * 4,
            jax.ShapeDtypeStruct((2, TOK), F32),
            jax.ShapeDtypeStruct((D, D), BF16),
            jax.ShapeDtypeStruct((D, D), BF16),
            jax.ShapeDtypeStruct((16, 256), BF16),
        ),
        in_specs=[smem, vmem, vmem] + [hbm] * 8,
        out_specs=(*[vmem] * 5, hbm, hbm, vmem),
        scratch_shapes=[
            V((TOK, D), BF16), V((TOK, D), BF16), V((TOK, D), BF16), V((D, D), BF16), V((16, TOK, TOK), F32), V((TOK, D), BF16),
            V((D, D), BF16), V((2, 2, 256, D), BF16), V((D, D), BF16), V((ALL, ALL), BF16), V((2, D, TOK), BF16),
            V((D, D), BF16), V((D, D), BF16), V((2, 2, TOK, D), BF16),
            V((2, ALL, TOK), BF16), V((2, ALL, TOK), BF16), V((2, TOK, ALL), BF16), V((2, 2, ALL, TOK), BF16),
            V((KC, NZ, ROWS, CW), BF16), V((KC, NZ, ROWS, CW), BF16), V((KC, NQ, ROWS, CW), BF16),
            V((2, KC, NP, ROWS, CW), BF16),
            V((4, BLK, D), F32), V((4, BLK, D), F32),
            V((KC, NP * ROWS, CW), BF16), V((KC, NP * ROWS, CW), BF16), V((NP * ROWS, 128), F32),
            V((4, 2, 4, ROWS, CW), BF16), V((4, 2, 4, ROWS, CW), BF16), V((4, 2, BLK, CW), F32),
            V((2, NP, ROWS, CW), BF16), V((2, NP, ROWS, CW), BF16),
            V((NQ, ROWS, CW), BF16), V((2, NZ, ROWS, CW), BF16), V((2, NZ, ROWS, CW), BF16),
            V((NP, 8, 128), F32), V((NP, 8, 128), F32), V((NQ, ROWS, 128), BF16),
            V((NZ, 8, 128), F32), V((NZ, 8, 128), F32), V((8, 128), F32), V((8, 128), F32),
            V((2, TOK, CW), BF16), V((2, TOK, CW), BF16),
            V((2, 2, NZ, NQ, 16, 128), BF16), V((2, NP, NZ, 16, 128), BF16),
            V((NZ, 16, 256), BF16), V((NZ, 16, 256), BF16),
            pltpu.SemaphoreType.DMA((8,)), pltpu.SemaphoreType.DMA((8,)), pltpu.SemaphoreType.DMA((2,)),
            *dma(7), *dma(KC, NZ), *dma(KC, NP), *dma(KC), *dma(4),
            *dma(2, NP), *dma(2, NZ), *dma(NP), *dma(NZ), *dma(2, NP), *dma(NZ),
        ],
        compiler_params=pltpu.CompilerParams(
            collective_id=0, has_side_effects=True, vmem_limit_bytes=62 * 1024 * 1024
        ),
        cost_estimate=pl.CostEstimate(flops=14_000_000_000, bytes_accessed=12_000_000, transcendentals=1_310_720),
    )(lengths, ids, gate, x, g, q, k, v, ap, w_in, w_out)


def on_device(
    mid_acts, out_grad, queries, key_rows, value_head_rows, seq_lengths,
    expert_ids, gate_probs, wide_in, wide_out, attn_proj,
):
    grad_mid, grad_q, grad_k, grad_v, grad_gates, grad_in, grad_out, proj = moe(
        seq_lengths, expert_ids.T, gate_probs.T, mid_acts, out_grad, queries, key_rows, value_head_rows, attn_proj,
        wide_in[0], wide_out[0],
    )
    return (grad_mid, grad_q, grad_k, grad_v, grad_gates.T, grad_in[None], grad_out[None], proj)


def solution(mesh):
    both = ("expert", "replica")
    return jax.shard_map(
        on_device,
        mesh=mesh,
        in_specs=(
            P(both, None), P(both, None), P(both, None), P(both, None), P(both, None), P(both),
            P(both, None), P(both, None), P("expert", None, "replica"), P("expert", "replica", None), P(),
        ),
        out_specs=(
            P(both, None), P(both, None), P(both, None), P(both, None), P(both, None),
            P("expert", None, "replica"), P("expert", "replica", None), P("expert", "replica"),
        ),
        check_vma=False,
    )
```

time: 175 us -> 139 us (0.79)
  Pallas kernels: 150 us -> 123 us
  matrix products: 7.04 us -> 0 us
  other arithmetic: 3.51 us -> 0 us
    pallas_call x1, Pallas kernels: 150 us -> 123 us  [moe(): pl.pallas_call(moe_kernel, out_shape=(*[jax.ShapeDtypeStruct((TOK, D), BF...]
    dot_general x6 -> x0, matrix products: 6.51 us -> none  [the longest x1 2.52 us: dot_nt(): lax.dot_general(a, b, (((1,), (1,)), ((), ())), preferred_element_type=F32)]
    unnamed x28 -> x16, local copies, waits for them, and re-layouts: 10.9 us -> 11.7 us
where the time goes in v2:
time: 139 us; the launch traced here: 136 us
  Pallas kernels  123 us (88%)
  local copies, waits for them, and re-layouts  11.7 us (8%)
    pallas_call x1, Pallas kernels, moe(): pl.pallas_call(moe_kernel, out_shape=(*[jax.ShapeDtypeStruct((TOK, D), BF...  123 us
    unnamed x16, local copies, waits for them, and re-layouts  11.7 us

profile of v2, /device:TPU:4, one launch (start us, length us, event | category | flops | bytes accessed | tf_op | source)
XLA Modules:
  0.0 136.4 jit_solution(13057229656580714642)
XLA Ops:
  1.3 123.4 %shard_map.170 = (bf16[128,1024]{1,0:T(8,128)(2,1)}, bf16[128,1024]{1,0:T(8,128)(2,1)}, bf16[128,1024]{1,0:T(8,128)(2,1)}, bf16[128,1024]{1,0:T(8,128)(2,1)}, f3...) custom-call(s32[1]{0:T(128)S(6)} %copy.27.length, ...), custom_call_target="tpu_custom_call" | custom-call | flops 14000000000 | bytes 12000000 | tf_op jit(solution)/shard_map/pallas_call | solution.py:563
  124.7 0.0 copy-start.3
  124.7 0.0 copy-start.1
  124.7 1.8 %copy.28 = bf16[128,1024]{1,0:T(8,128)(2,1)} copy(bf16[128,1024]{1,0:T(8,128)(2,1)} %get-tuple-element.32) | data formatting | bytes 524288
  126.5 1.7 %copy.29 = bf16[128,1024]{1,0:T(8,128)(2,1)} copy(bf16[128,1024]{1,0:T(8,128)(2,1)} %get-tuple-element.33) | data formatting | bytes 524288
  128.2 1.7 %copy.30 = bf16[128,1024]{1,0:T(8,128)(2,1)} copy(bf16[128,1024]{1,0:T(8,128)(2,1)} %get-tuple-element.34) | data formatting | bytes 524288
  129.9 1.7 %copy.31 = bf16[128,1024]{1,0:T(8,128)(2,1)} copy(bf16[128,1024]{1,0:T(8,128)(2,1)} %get-tuple-element.35) | data formatting | bytes 524288
  131.5 0.0 copy-done.3
  131.5 0.6 copy.32
  132.1 0.0 copy-done.1
  132.1 0.0 copy-start
  132.1 1.3 copy.33
  133.4 1.0 copy-done
  134.4 0.0 copy-start.2
  134.4 1.3 copy.34
  135.8 0.0 copy-done.2
  135.8 0.6 copy.35
Async XLA Ops:
  124.7 6.8 %copy-start.3 = (f32[2,128]{1,0:T(2,128)S(1)}, f32[2,128]{1,0:T(2,128)}, u32[]{:S(2)}) copy-start(f32[2,128]{1,0:T(2,128)} %get-tuple-element.20) | copy-start | bytes 3076
  124.7 7.4 %copy-start.1 = (bf16[1024,1024]{1,0:T(8,128)(2,1)S(1)}, bf16[1024,1024]{1,0:T(8,128)(2,1)}, u32[]{:S(2)}) copy-start(bf16[1024,1024]{1,0:T(8,128)(2,1)} %get-tuple-element.21) | copy-start | bytes 6291460
  132.1 2.3 %copy-start = (bf16[1024,1024]{1,0:T(8,128)(2,1)S(1)}, bf16[1024,1024]{1,0:T(8,128)(2,1)}, u32[]{:S(2)}) copy-start(bf16[1024,1024]{1,0:T(8,128)(2,1)} %get-tuple-element.22) | copy-start | bytes 6291460
  134.4 1.3 copy-start.2

commit v3 on v2

--- a/solution.py
+++ b/solution.py
@@ -1,3 +1,4 @@
+import functools
 import math
 
 import jax
@@ -49,7 +50,6 @@
     e = lax.axis_index("expert")
     r = lax.axis_index("replica")
     z, q, xh, c = e // NQ, e % NQ, r // 2, r % 2
-    pm = xh * NQ + q
     other = 1 - c
     partner = (e, xh * 2 + other)
     late = []
@@ -58,7 +58,15 @@
         return (((z + j) % NZ) * NQ + q, r)
 
     def plane_of(j):
-        return (pm + j) % NP
+        i, n = j // 4, j % 4
+        x = (xh * 2 + q // 4 + n) % 4
+        return x // 2 * NQ + x % 2 * 4 + (q + n + i) % 4
+
+    def back(j):
+        return (4 - j // 4) % 4 * 4 + (4 - j % 4) % 4
+
+    def twin(j):
+        return (j // 4 + 2) % 4 * 4 + (j % 4 + 2) % 4
 
     def dev_p(j):
         p = plane_of(j)
@@ -156,18 +164,20 @@
     pair(1, xg.at[c, other], xg.at[c, other]).wait_recv()
 
     def copy_a(k, j):
-        return remote(sa.at[k, j], ra.at[k, (NZ - j) % NZ], a_ss.at[k, j], a_rs.at[k, (NZ - j) % NZ], dev_z(j))
-
-    def recv_a(k, j):
-        return remote(sa.at[k, j], ra.at[k, j], a_ss.at[k, j], a_rs.at[k, j], dev_z(j))
+        return remote(sa.at[k, j], ra.at[k, (NZ - j) % NZ], a_ss.at[k], a_rs.at[k], dev_z(j))
+
+    def recv_a(k):
+        group = ra.at[k, pl.ds(1, NZ - 1)]
+        return remote(group, group, a_ss.at[k], a_rs.at[k], dev_z(1))
 
     def copy_b(k, j):
         return remote(
-            sb.at[k, plane_of(j) % NQ], rr.at[c, k, (NP - j) % NP], b_ss.at[k, j], b_rs.at[k, (NP - j) % NP], dev_p(j)
+            sb.at[k, plane_of(j) % NQ], rr.at[c, k, back(j)], b_ss.at[k], b_rs.at[k], dev_p(j)
         )
 
-    def recv_b(k, j):
-        return remote(sb.at[k, 0], rr.at[c, k, j], b_ss.at[k, j], b_rs.at[k, j], dev_p(j))
+    def recv_b(k):
+        group = rr.at[c, k, pl.ds(1, NP - 1)]
+        return remote(group, group, b_ss.at[k], b_rs.at[k], dev_p(1))
 
     def copy_c(k):
         return remote(rr.at[c, k], rr.at[c, k], c_ss.at[k], c_rs.at[k], partner)
@@ -221,7 +231,7 @@
     late.append(x_copy.wait_send)
 
     def stage_b(k):
-        each(NZ, lambda j: recv_a(k, j).wait_recv())
+        recv_a(k).wait_recv()
         if k + AHEAD < KC:
             stage_a(k + AHEAD)
         rows = dot_nn(swap[...], ra[k].reshape(ALL, CW))
@@ -230,7 +240,7 @@
         rr[c, k, 0] = sb[k, q]
 
     def stage_c(k):
-        each(NP, lambda j: recv_b(k, j).wait_recv())
+        recv_b(k).wait_recv()
         copy_c(k).start()
 
     def stage_d(k):
@@ -266,8 +276,8 @@
             for copy in arranged:
                 copy.wait()
     for k in range(KC):
-        late.append(lambda k=k: each(NZ, lambda j: recv_a(k, j).wait_send()))
-        late.append(lambda k=k: each(NP, lambda j: recv_b(k, j).wait_send()))
+        late.append(lambda k=k: recv_a(k).wait_send())
+        late.append(lambda k=k: recv_b(k).wait_send())
         late.append(copy_c(k).wait_send)
 
     SUB = 32
@@ -312,16 +322,18 @@
             do[i, h] = part(c, h)
 
     def copy_br(h, j):
-        return remote(sbr.at[h, j], rbr.at[h, (NP - j) % NP], br_ss.at[h, j], br_rs.at[h, (NP - j) % NP], dev_p(j))
-
-    def recv_br(h, j):
-        return remote(sbr.at[h, j], rbr.at[h, j], br_ss.at[h, j], br_rs.at[h, j], dev_p(j))
+        return remote(sbr.at[h, j], rbr.at[h, back(j)], br_ss.at[h], br_rs.at[h], dev_p(j))
+
+    def recv_br(h):
+        group = rbr.at[h, pl.ds(1, NP - 1)]
+        return remote(group, group, br_ss.at[h], br_rs.at[h], dev_p(1))
 
     def copy_sp(j):
-        return remote(sp.at[j], sp_in.at[(NP - j) % NP], sp_ss.at[j], sp_rs.at[(NP - j) % NP], dev_p(j))
-
-    def recv_sp(j):
-        return remote(sp.at[j], sp_in.at[j], sp_ss.at[j], sp_rs.at[j], dev_p(j))
+        return remote(sp.at[j], sp_in.at[back(j)], sp_ss, sp_rs, dev_p(j))
+
+    def recv_sp():
+        group = sp_in.at[pl.ds(1, NP - 1)]
+        return remote(group, group, sp_ss, sp_rs, dev_p(1))
 
     diagonal = lax.broadcasted_iota(jnp.int32, (ROWS, 128), 0) == lax.broadcasted_iota(jnp.int32, (ROWS, 128), 1)
 
@@ -353,8 +365,8 @@
     for i in range(4):
         side_block(i)
     for h in range(2):
-        late.append(lambda h=h: each(NP, lambda j: recv_br(h, j).wait_send()))
-    late.append(lambda: each(NP, lambda j: recv_sp(j).wait_send()))
+        late.append(lambda h=h: recv_br(h).wait_send())
+    late.append(lambda: recv_sp().wait_send())
 
     def wide_in_body(n, _):
         at = pl.multiple_of((n // KC) * CW, CW)
@@ -372,11 +384,6 @@
         grad_out[pl.ds(pl.multiple_of(f * CW, CW), CW), pl.ds(pl.multiple_of(k * CW, CW), CW)] = term
         return 0
 
-    lax.fori_loop(0, KC * KC, wide_in_body, 0)
-    out_in = pltpu.make_async_copy(grad_in, gin_hbm, o_sem.at[0])
-    out_in.start()
-    late.append(out_in.wait)
-
     for j in range(2):
         t = t_buf[j].astype(F32)
         t_all[j] = jnp.where(t != 0.0, 1.0, 0.0).T.astype(BF16)
@@ -384,37 +391,39 @@
         t_one[j, 1] = jnp.where(t < 0.0, 1.0, 0.0).astype(BF16)
 
     def copy_ar(h, j):
-        return remote(sar.at[h, j], rar.at[h, (NZ - j) % NZ], ar_ss.at[h, j], ar_rs.at[h, (NZ - j) % NZ], dev_z(j))
-
-    def recv_ar(h, j):
-        return remote(sar.at[h, j], rar.at[h, j], ar_ss.at[h, j], ar_rs.at[h, j], dev_z(j))
+        return remote(sar.at[h, j], rar.at[h, (NZ - j) % NZ], ar_ss.at[h], ar_rs.at[h], dev_z(j))
+
+    def recv_ar(h):
+        group = rar.at[h, pl.ds(1, NZ - 1)]
+        return remote(group, group, ar_ss.at[h], ar_rs.at[h], dev_z(1))
 
     def copy_sz(j):
-        return remote(sz.at[j], sz_in.at[(NZ - j) % NZ], sz_ss.at[j], sz_rs.at[(NZ - j) % NZ], dev_z(j))
-
-    def recv_sz(j):
-        return remote(sz.at[j], sz_in.at[j], sz_ss.at[j], sz_rs.at[j], dev_z(j))
+        return remote(sz.at[j], sz_in.at[(NZ - j) % NZ], sz_ss, sz_rs, dev_z(j))
+
+    def recv_sz():
+        group = sz_in.at[pl.ds(1, NZ - 1)]
+        return remote(group, group, sz_ss, sz_rs, dev_z(1))
 
     def stage_z(h):
-        each(NP, lambda j: recv_br(h, j).wait_recv())
+        recv_br(h).wait_recv()
         for j in range(NQ):
             one = sbr if j == 0 else rbr
-            yy[(q + j) % NQ] = (one[h, j].astype(F32) + rbr[h, j + NQ].astype(F32)).astype(BF16)
+            yy[plane_of(j) % NQ] = (one[h, j].astype(F32) + rbr[h, twin(j)].astype(F32)).astype(BF16)
         sar[h] = dot_nn(swap[...], yy[...].reshape(ALL, CW)).astype(BF16).reshape(NZ, ROWS, CW)
         each(NZ, lambda j: copy_ar(h, j).start())
         rar[h, 0] = sar[h, 0]
-        late.append(lambda: each(NZ, lambda j: recv_ar(h, j).wait_send()))
+        late.append(lambda: recv_ar(h).wait_send())
 
     lanes = lax.broadcasted_iota(jnp.int32, (ROWS, 128), 1)
 
     def side_z():
-        each(NP, lambda j: recv_sp(j).wait_recv())
+        recv_sp().wait_recv()
         for j in range(NQ):
             one = sp if j == 0 else sp_in
-            row = (one[j] + sp_in[j + NQ])[0:1, :]
+            row = (one[j] + sp_in[twin(j)])[0:1, :]
             s = jnp.sum(jnp.where(diagonal, jnp.broadcast_to(row, (ROWS, 128)), 0.0), axis=1, keepdims=True)
             hi = s.astype(BF16).astype(F32)
-            ys[(q + j) % NQ] = jnp.where(lanes == 0, hi, jnp.where(lanes == 1, s - hi, 0.0)).astype(BF16)
+            ys[plane_of(j) % NQ] = jnp.where(lanes == 0, hi, jnp.where(lanes == 1, s - hi, 0.0)).astype(BF16)
         back = dot_nn(swap[...], ys[...].reshape(ALL, 128))
         for n in range(NZ):
             s = jnp.sum(back[n * ROWS : (n + 1) * ROWS, :], axis=1, keepdims=True)
@@ -422,34 +431,35 @@
             sz[n] = jnp.broadcast_to(row, (8, 128))
         each(NZ, lambda j: copy_sz(j).start())
         sz_in[0] = sz[0]
-        late.append(lambda: each(NZ, lambda j: recv_sz(j).wait_send()))
+        late.append(lambda: recv_sz().wait_send())
 
     stage_z(0)
-    lax.fori_loop(0, KC * KC // 2, wide_out_body, 0)
+    lax.fori_loop(0, KC * KC // 2, wide_in_body, 0)
     stage_z(1)
     side_z()
-    lax.fori_loop(KC * KC // 2, KC * KC, wide_out_body, 0)
-    out_out = pltpu.make_async_copy(grad_out, gout_hbm, o_sem.at[1])
-    out_out.start()
-    late.append(out_out.wait)
+    lax.fori_loop(KC * KC // 2, KC * KC, wide_in_body, 0)
+    out_in = pltpu.make_async_copy(grad_in, gin_hbm, o_sem.at[0])
+    out_in.start()
+    late.append(out_in.wait)
     pair(2, xg.at[other, other], xg.at[other, other]).wait_recv()
     pair(3, mixt.at[other], mixt.at[other]).wait_recv()
 
     def copy_p2(h, j):
         p = plane_of(j)
         return remote(
-            rs_b.at[h, p // NQ, :, p % NQ], rs2.at[h, (NP - j) % NP], p2_ss.at[h, j], p2_rs.at[h, (NP - j) % NP],
+            rs_b.at[h, p // NQ, :, p % NQ], rs2.at[h, back(j)], p2_ss.at[h], p2_rs.at[h],
             dev_p(j),
         )
 
-    def recv_p2(h, j):
-        return remote(rs_b.at[h, 0, :, 0], rs2.at[h, j], p2_ss.at[h, j], p2_rs.at[h, j], dev_p(j))
+    def recv_p2(h):
+        group = rs2.at[h, pl.ds(1, NP - 1)]
+        return remote(group, group, p2_ss.at[h], p2_rs.at[h], dev_p(1))
 
     def mo_copy(h):
         return pair(4 + h, mo.at[h], mo_in.at[h])
 
     def home(h):
-        each(NZ, lambda j: recv_ar(h, j).wait_recv())
+        recv_ar(h).wait_recv()
         rows = rar[h].reshape(ALL, CW)
         theirs = dot_nn(t_all[other], rows)
         ours = dot_nn(t_all[c], rows)
@@ -468,10 +478,15 @@
             rs_b[h, xhi] = part.astype(BF16).reshape(NZ, NQ, 16, 128)
         each(NP, lambda j: copy_p2(h, j).start())
         rs2[h, 0] = rs_b[h, xh, :, q]
-        late.append(lambda: each(NP, lambda j: recv_p2(h, j).wait_send()))
+        late.append(lambda: recv_p2(h).wait_send())
 
     home(0)
+    lax.fori_loop(0, KC * KC // 2, wide_out_body, 0)
     home(1)
+    lax.fori_loop(KC * KC // 2, KC * KC, wide_out_body, 0)
+    out_out = pltpu.make_async_copy(grad_out, gout_hbm, o_sem.at[1])
+    out_out.start()
+    late.append(out_out.wait)
 
     for h in range(2):
         mo_copy(h).wait_recv()
@@ -502,23 +517,24 @@
     lax.fori_loop(0, 4, backward, 0)
 
     for h in range(2):
-        each(NP, lambda j: recv_p2(h, j).wait_recv())
+        recv_p2(h).wait_recv()
         total = lax.fori_loop(1, NP, lambda j, t: t + rs2[h, j].astype(F32), rs2[h, 0].astype(F32))
         rs_c[:, :, h * 128 : (h + 1) * 128] = total.astype(BF16)
 
     def copy_p3(j):
         return remote(
-            rs_c.at[(z + j) % NZ], rs3.at[(NZ - j) % NZ], p3_ss.at[j], p3_rs.at[(NZ - j) % NZ], dev_z(j)
+            rs_c.at[(z + j) % NZ], rs3.at[(NZ - j) % NZ], p3_ss, p3_rs, dev_z(j)
         )
 
-    def recv_p3(j):
-        return remote(rs_c.at[0], rs3.at[j], p3_ss.at[j], p3_rs.at[j], dev_z(j))
+    def recv_p3():
+        group = rs3.at[pl.ds(1, NZ - 1)]
+        return remote(group, group, p3_ss, p3_rs, dev_z(1))
 
     each(NZ, lambda j: copy_p3(j).start())
     rs3[0] = rs_c[z]
-    late.append(lambda: each(NZ, lambda j: recv_p3(j).wait_send()))
-
-    each(NZ, lambda j: recv_sz(j).wait_recv())
+    late.append(lambda: recv_p3().wait_send())
+
+    recv_sz().wait_recv()
     row16 = lax.broadcasted_iota(jnp.int32, (16, 128), 0)
 
     def gate_terms(j):
@@ -544,7 +560,7 @@
     for k in range(2):
         gates[k : k + 1, :] = (ours[k : k + 1, :] + ga_in[k : k + 1, :]) / gate[k]
 
-    each(NZ, lambda j: recv_p3(j).wait_recv())
+    recv_p3().wait_recv()
     proj[...] = jnp.sum(rs3[...].astype(F32), axis=0).astype(BF16)
 
     for wait in late:
@@ -589,8 +605,8 @@
             V((2, 2, NZ, NQ, 16, 128), BF16), V((2, NP, NZ, 16, 128), BF16),
             V((NZ, 16, 256), BF16), V((NZ, 16, 256), BF16),
             pltpu.SemaphoreType.DMA((8,)), pltpu.SemaphoreType.DMA((8,)), pltpu.SemaphoreType.DMA((2,)),
-            *dma(7), *dma(KC, NZ), *dma(KC, NP), *dma(KC), *dma(4),
-            *dma(2, NP), *dma(2, NZ), *dma(NP), *dma(NZ), *dma(2, NP), *dma(NZ),
+            *dma(7), *dma(KC), *dma(KC), *dma(KC), *dma(4),
+            *dma(2), *dma(2), *dma(), *dma(), *dma(2), *dma(),
         ],
         compiler_params=pltpu.CompilerParams(
             collective_id=0, has_side_effects=True, vmem_limit_bytes=62 * 1024 * 1024
@@ -599,14 +615,48 @@
     )(lengths, ids, gate, x, g, q, k, v, ap, w_in, w_out)
 
 
+def place_kernel(count, *refs):
+    src, dst, held = refs[:count], refs[count : 2 * count], refs[2 * count : 3 * count]
+    in_sem, out_sem = refs[3 * count :]
+    loads, stores = [], []
+    for n in range(count):
+        rows = src[n].shape[0]
+        pieces = 4 if rows == D else 1
+        for m in range(pieces):
+            at = pl.ds(m * (rows // pieces), rows // pieces)
+            loads.append(pltpu.make_async_copy(src[n].at[at], held[n].at[at], in_sem.at[len(loads)]))
+            stores.append(pltpu.make_async_copy(held[n].at[at], dst[n].at[at], out_sem.at[len(stores)]))
+    for load in loads:
+        load.start()
+    for load, store in zip(loads, stores):
+        load.wait()
+        store.start()
+    for store in stores:
+        store.wait()
+
+
+def place(arrays):
+    hbm = pl.BlockSpec(memory_space=pl.ANY)
+    count = len(arrays)
+    return pl.pallas_call(
+        functools.partial(place_kernel, count),
+        out_shape=tuple(jax.ShapeDtypeStruct(a.shape, a.dtype) for a in arrays),
+        in_specs=[hbm] * count,
+        out_specs=(hbm,) * count,
+        scratch_shapes=[pltpu.VMEM(a.shape, a.dtype) for a in arrays]
+        + [pltpu.SemaphoreType.DMA((count + 6,)), pltpu.SemaphoreType.DMA((count + 6,))],
+    )(*arrays)
+
+
 def on_device(
     mid_acts, out_grad, queries, key_rows, value_head_rows, seq_lengths,
     expert_ids, gate_probs, wide_in, wide_out, attn_proj,
 ):
-    grad_mid, grad_q, grad_k, grad_v, grad_gates, grad_in, grad_out, proj = moe(
+    results = moe(
         seq_lengths, expert_ids.T, gate_probs.T, mid_acts, out_grad, queries, key_rows, value_head_rows, attn_proj,
         wide_in[0], wide_out[0],
     )
+    grad_mid, grad_q, grad_k, grad_v, grad_gates, grad_in, grad_out, proj = place(results)
     return (grad_mid, grad_q, grad_k, grad_v, grad_gates.T, grad_in[None], grad_out[None], proj)
 
 

time: 139 us -> 121 us (0.87)
  local copies, waits for them, and re-layouts: 11.7 us -> 0 us
  Pallas kernels: 123 us -> 118 us
    unnamed x16 -> x0, local copies, waits for them, and re-layouts: 11.7 us -> none
    pallas_call x1, Pallas kernels: 123 us -> 113 us  [moe(): pl.pallas_call(moe_kernel, out_shape=(*[jax.ShapeDtypeStruct((TOK, D), BF...]
    pallas_call x0 -> x1, Pallas kernels: none -> 4.84 us  [place(): pl.pallas_call(functools.partial(place_kernel, count), out_shape=tuple((j...]
where the time goes in v3:
time: 121 us; the launch traced here: 120 us
  Pallas kernels  118 us (98%)
  between operations  1.29 us (1%)
    pallas_call x1, Pallas kernels, moe(): pl.pallas_call(moe_kernel, out_shape=(*[jax.ShapeDtypeStruct((TOK, D), BF...  113 us
    pallas_call x1, Pallas kernels, place(): pl.pallas_call(functools.partial(place_kernel, count), out_shape=tuple((j...  4.84 us

profile of v3, /device:TPU:4, one launch (start us, length us, event | category | flops | bytes accessed | tf_op | source)
XLA Modules:
  0.0 119.5 jit_solution(16177678675579742854)
XLA Ops:
  1.3 113.4 %shard_map.170 = (bf16[128,1024]{1,0:T(8,128)(2,1)}, bf16[128,1024]{1,0:T(8,128)(2,1)}, bf16[128,1024]{1,0:T(8,128)(2,1)}, bf16[128,1024]{1,0:T(8,128)(2,1)}, f3...) custom-call(s32[1]{0:T(128)S(6)} %copy.19.length, ...), custom_call_target="tpu_custom_call" | custom-call | flops 14000000000 | bytes 12000000 | tf_op jit(solution)/shard_map/pallas_call | solution.py:579
  114.7 4.8 %shard_map.171 = (bf16[128,1024]{1,0:T(8,128)(2,1)}, bf16[128,1024]{1,0:T(8,128)(2,1)}, bf16[128,1024]{1,0:T(8,128)(2,1)}, bf16[128,1024]{1,0:T(8,128)(2,1)}, f3...) custom-call(bf16[128,1024]{1,0:T(8,128)(2,1)} %get-tuple-element.24.refs_0_, ...), custom_call_target="tpu_custom_call" | custom-call | tf_op jit(solution)/shard_map/pallas_call | solution.py:641

commit v4 on v3

--- a/solution.py
+++ b/solution.py
@@ -42,7 +42,7 @@
     mid, grad_q, grad_k, grad_v, gates, gin_hbm, gout_hbm, proj,
     q_buf, k_buf, v_buf, ap, probs, d_heads,
     w_in, w_arr, w_out, swap, mixt, grad_in, grad_out, xg, t_buf, t_use, t_all, t_one, sa, ra, sb, rr,
-    pre, dact, act, dpre, side, ds, dr, do, sbr, rbr, yy, sar, rar,
+    pre, dact, act, dpre, xt, side, ds, dr, do, sbr, rbr, yy, sar, rar,
     sp, sp_in, ys, sz, sz_in, ga, ga_in, mo, mo_in, rs_b, rs2, rs_c, rs3,
     w_sem, n_sem, o_sem, pair_ss, pair_rs, a_ss, a_rs, b_ss, b_rs, c_ss, c_rs, cr_ss, cr_rs,
     br_ss, br_rs, ar_ss, ar_rs, sp_ss, sp_rs, sz_ss, sz_rs, p2_ss, p2_rs, p3_ss, p3_rs,
@@ -219,16 +219,13 @@
 
     for copy in heads_in:
         copy.wait()
-    lax.fori_loop(0, 8, forward, 0)
+    lax.fori_loop(0, 3, forward, 0)
 
     row = lax.broadcasted_iota(jnp.int32, (8, ALL), 1)
     place = (row % (NQ * CAP)) // CAP * ROWS + (row % ROWS) // (NQ * CAP) * (NQ * CAP) + row // ROWS * CAP + row % CAP
     for n in range(8):
         rows = lax.broadcasted_iota(jnp.int32, (ROWS, ALL), 0) + n * ROWS
         swap[n * ROWS : (n + 1) * ROWS, :] = jnp.where(rows == place[0:1, :], 1.0, 0.0).astype(BF16)
-    x_copy = pair(3, mixt.at[c], mixt.at[c])
-    x_copy.start()
-    late.append(x_copy.wait_send)
 
     def stage_b(k):
         recv_a(k).wait_recv()
@@ -249,24 +246,33 @@
             loads[0].wait()
             loads[1].wait()
 
-        def body(i, _):
-            xk = rr[0, k, pl.ds(4 * i, 4)].reshape(BLK, CW)
-            gk = rr[1, k, pl.ds(4 * i, 4)].reshape(BLK, CW)
-            p_new = dot_nn(xk, w_in[k * CW : (k + 1) * CW, :])
-            d_new = dot_nt(gk, w_out[:, k * CW : (k + 1) * CW])
-            if k == 0:
-                pre[i] = p_new
-                dact[i] = d_new
-            else:
-                pre[i] += p_new
-                dact[i] += d_new
-            return 0
-
-        lax.fori_loop(0, 4, body, 0)
+        if k < KC - 1:
+            lax.fori_loop(0, 4, lambda i, _: d_block(k, i), 0)
+            xt[k] = rr[0, k].reshape(NP * ROWS, CW).T
+
+    def d_block(k, i):
+        xk = rr[0, k, pl.ds(4 * i, 4)].reshape(BLK, CW)
+        gk = rr[1, k, pl.ds(4 * i, 4)].reshape(BLK, CW)
+        p_new = dot_nn(xk, w_in[k * CW : (k + 1) * CW, :])
+        d_new = dot_nt(gk, w_out[:, k * CW : (k + 1) * CW])
+        if k == 0:
+            pre[i] = p_new
+            dact[i] = d_new
+        else:
+            pre[i] += p_new
+            dact[i] += d_new
+        return 0
 
     for step in range(KC + 2):
         if step < KC:
             stage_b(step)
+        if step in (1, 2):
+            lax.fori_loop(2 * step + 1, 2 * step + 3, forward, 0)
+        if step == 3:
+            forward(7, 0)
+            x_copy = pair(3, mixt.at[c], mixt.at[c])
+            x_copy.start()
+            late.append(x_copy.wait_send)
         if 0 <= step - 1 < KC:
             stage_c(step - 1)
         if 0 <= step - 2 < KC:
@@ -356,32 +362,29 @@
 
     for i in range(5):
         if i < 4:
+            d_block(KC - 1, i)
             gelu_block(i)
             dx_block(i)
         if i > 0:
             return_block(i - 1, 0)
     for i in range(4):
         return_block(i, 1)
-    for i in range(4):
-        side_block(i)
     for h in range(2):
         late.append(lambda h=h: recv_br(h).wait_send())
     late.append(lambda: recv_sp().wait_send())
 
-    def wide_in_body(n, _):
-        at = pl.multiple_of((n // KC) * CW, CW)
-        f = n % KC
-        rows = rr[0, n // KC].reshape(NP * ROWS, CW)
-        term = dot_tn(rows, dpre[f]).astype(BF16)
-        grad_in[pl.ds(at, CW), pl.ds(pl.multiple_of(f * CW, CW), CW)] = term
+    def wide_in_body(k, _):
+        at = pl.multiple_of(k * CW, CW)
+        for f in range(KC):
+            grad_in[pl.ds(at, CW), f * CW : (f + 1) * CW] = dot_nn(xt[k], dpre[f]).astype(BF16)
         return 0
 
-    def wide_out_body(n, _):
-        f = n // KC
-        k = n % KC
-        rows = rr[1, k].reshape(NP * ROWS, CW)
-        term = dot_tn(act[f], rows).astype(BF16)
-        grad_out[pl.ds(pl.multiple_of(f * CW, CW), CW), pl.ds(pl.multiple_of(k * CW, CW), CW)] = term
+    def wide_out_body(f, _):
+        at = pl.multiple_of(f * CW, CW)
+        rows = act[f].T
+        for k in range(KC):
+            term = dot_nn(rows, rr[1, k].reshape(NP * ROWS, CW)).astype(BF16)
+            grad_out[pl.ds(at, CW), k * CW : (k + 1) * CW] = term
         return 0
 
     for j in range(2):
@@ -434,10 +437,13 @@
         late.append(lambda: recv_sz().wait_send())
 
     stage_z(0)
-    lax.fori_loop(0, KC * KC // 2, wide_in_body, 0)
+    for i in range(4):
+        side_block(i)
+    lax.fori_loop(0, 2, wide_in_body, 0)
     stage_z(1)
     side_z()
-    lax.fori_loop(KC * KC // 2, KC * KC, wide_in_body, 0)
+    xt[3] = rr[0, 3].reshape(NP * ROWS, CW).T
+    lax.fori_loop(2, 4, wide_in_body, 0)
     out_in = pltpu.make_async_copy(grad_in, gin_hbm, o_sem.at[0])
     out_in.start()
     late.append(out_in.wait)
@@ -481,9 +487,9 @@
         late.append(lambda: recv_p2(h).wait_send())
 
     home(0)
-    lax.fori_loop(0, KC * KC // 2, wide_out_body, 0)
+    lax.fori_loop(0, 2, wide_out_body, 0)
     home(1)
-    lax.fori_loop(KC * KC // 2, KC * KC, wide_out_body, 0)
+    lax.fori_loop(2, 4, wide_out_body, 0)
     out_out = pltpu.make_async_copy(grad_out, gout_hbm, o_sem.at[1])
     out_out.start()
     late.append(out_out.wait)
@@ -595,7 +601,7 @@
             V((KC, NZ, ROWS, CW), BF16), V((KC, NZ, ROWS, CW), BF16), V((KC, NQ, ROWS, CW), BF16),
             V((2, KC, NP, ROWS, CW), BF16),
             V((4, BLK, D), F32), V((4, BLK, D), F32),
-            V((KC, NP * ROWS, CW), BF16), V((KC, NP * ROWS, CW), BF16), V((NP * ROWS, 128), F32),
+            V((KC, NP * ROWS, CW), BF16), V((KC, NP * ROWS, CW), BF16), V((KC, CW, NP * ROWS), BF16), V((NP * ROWS, 128), F32),
             V((4, 2, 4, ROWS, CW), BF16), V((4, 2, 4, ROWS, CW), BF16), V((4, 2, BLK, CW), F32),
             V((2, NP, ROWS, CW), BF16), V((2, NP, ROWS, CW), BF16),
             V((NQ, ROWS, CW), BF16), V((2, NZ, ROWS, CW), BF16), V((2, NZ, ROWS, CW), BF16),

time: 121 us -> 120 us (level); the launches traced: 120 us -> 120 us
  no operation moved by 1% of the time
where the time goes in v4:
time: 120 us
  Pallas kernels  119 us (99%)
  between operations  1.45 us (1%)
    pallas_call x1, Pallas kernels, moe(): pl.pallas_call(moe_kernel, out_shape=(*[jax.ShapeDtypeStruct((TOK, D), BF...  114 us
    pallas_call x1, Pallas kernels, place(): pl.pallas_call(functools.partial(place_kernel, count), out_shape=tuple((j...  4.84 us

profile of v4, /device:TPU:4, one launch (start us, length us, event | category | flops | bytes accessed | tf_op | source)
XLA Modules:
  0.0 120.3 jit_solution(15256193308122200165)
XLA Ops:
  1.3 114.0 %shard_map.170 = (bf16[128,1024]{1,0:T(8,128)(2,1)}, bf16[128,1024]{1,0:T(8,128)(2,1)}, bf16[128,1024]{1,0:T(8,128)(2,1)}, bf16[128,1024]{1,0:T(8,128)(2,1)}, f3...) custom-call(s32[1]{0:T(128)S(6)} %copy.19.length, ...), custom_call_target="tpu_custom_call" | custom-call | flops 14000000000 | bytes 12000000 | tf_op jit(solution)/shard_map/pallas_call | solution.py:585
  115.3 4.8 %shard_map.171 = (bf16[128,1024]{1,0:T(8,128)(2,1)}, bf16[128,1024]{1,0:T(8,128)(2,1)}, bf16[128,1024]{1,0:T(8,128)(2,1)}, bf16[128,1024]{1,0:T(8,128)(2,1)}, f3...) custom-call(bf16[128,1024]{1,0:T(8,128)(2,1)} %get-tuple-element.24.refs_0_, ...), custom_call_target="tpu_custom_call" | custom-call | tf_op jit(solution)/shard_map/pallas_call | solution.py:647
